TPU v7x, 512 devices: a whole 4x8x8 slice. The times are simulated.
512 devices in a mesh: own: 32 (over y, z_hi), blk: 16 (over x, z_lo, core).
Axes of the slice: x: 4, y: 8, z: 8 (z_hi: 4, z_lo: 2; z = z_hi * 2 + z_lo), core: 2. Of those that a mesh axis runs over, the one named last changes fastest.
Arguments:
- points: bfloat16 [64, 65536], P(None, ('own', 'blk')), may hold values from -6 to 6
- solution_field: float32 [33, 65536], P(None, ('own', 'blk')), may hold values from -6 to 6
- residual: float32 [33, 65536], P(None, ('own', 'blk')), may hold values from -12 to 12
- direction: float32 [33, 65536], P(None, ('own', 'blk')), may hold values from -12 to 12
Outputs:
- solution_next: float32 [33, 65536], P(None, ('own', 'blk'))
- residual_next: float32 [33, 65536], P(None, ('own', 'blk'))
- direction_next: float32 [33, 65536], P(None, ('own', 'blk'))
All inputs are finite; a program needn't handle non-finite values.
Results may differ from a plain program's by a relative error of at most 0.0027.
Values may be sent and summed in bfloat16 or wider, within the bound.
No kernel may reach another device: no remote copies, remote signals or barrier semaphores. Data moves between devices by JAX's collectives and lax.ppermute only.
A program may use at most 64 MiB of HBM per device.

v0:
```python
import functools
import math

import jax
import jax.numpy as jnp
from jax import lax
from jax.sharding import Mesh
from jax.sharding import PartitionSpec as P

OWN = ("own_0", "own_1")
BLK = ("blk_0", "blk_1", "blk_2")
OWN_BLK = ("own_0", "own_1", "blk_0", "blk_1", "blk_2")


amplitude = 1.0
decay_rate = 1.0 / 16.0
noise_level = 0.5


def joined_along(pieces, dim):
    shape = list(pieces.shape[1:])
    shape[dim] *= pieces.shape[0]
    return jnp.moveaxis(pieces, 0, dim).reshape(shape)


def copy_for_each(shard, axis):
    peers = lax.axis_size(axis)
    return lax.all_to_all(
        jnp.broadcast_to(shard[None], (peers, *shard.shape)), axis, 0, 0, tiled=True
    )


def gather_directly(shard, axis, dim):
    return joined_along(copy_for_each(shard, axis), dim)


def in_one_piece(arrays, axis, dim, along):
    widths = [a.shape[along] for a in arrays]
    both = jnp.concatenate(arrays, axis=along)
    filled = lax.all_gather(both, axis, axis=dim, tiled=True)
    return tuple(jnp.split(filled, [sum(widths[:k]) for k in range(1, len(widths))], axis=along))


def in_blocks(shard, dim, peers):
    before, after = (shard.shape[:dim], shard.shape[dim + 1 :])
    return jnp.moveaxis(shard.reshape(*before, peers, -1, *after), dim, 0)


def summed_on_arrival(shard, axis, dim):
    pieces = in_blocks(shard, dim, lax.axis_size(axis))
    arrived = lax.all_to_all(pieces, axis, split_axis=0, concat_axis=0, tiled=True)
    return arrived.sum(axis=0)


def one_axis_at_a_time(shard, axes):
    return functools.reduce(lax.psum, axes, shard)


def tile_products(row_blocks, row_norms, columns, dirs):
    col_norms = jnp.sum(jnp.square(columns.astype(jnp.float32)), axis=0)

    def single(pair):
        rows, norms = pair
        inner = lax.dot_general(
            rows, columns, (((0,), (0,)), ((), ())), preferred_element_type=jnp.float32
        )
        dist = jnp.maximum(norms[:, None] + col_norms[None, :] - 2.0 * inner, 0.0)
        kern = (amplitude * jnp.exp(-decay_rate * dist)).astype(jnp.bfloat16)
        return lax.dot_general(
            dirs, kern, (((1,), (1,)), ((), ())), preferred_element_type=jnp.float32
        )

    return lax.map(single, (row_blocks, row_norms))


def split_rows(rows):
    width = rows.shape[1]
    size = math.gcd(width, 512)
    count = width // size
    blocks = rows.reshape(rows.shape[0], count, size).transpose(1, 0, 2)
    norms = jnp.sum(jnp.square(blocks.astype(jnp.float32)), axis=1)
    return (blocks, norms)


def local(points, solution_field, residual, direction):
    dir_low = direction.astype(jnp.bfloat16)
    count_rhs = direction.shape[0]
    rows = gather_directly(points, OWN, 1)
    blocks, norms = split_rows(rows)
    piece = in_one_piece((points, dir_low), BLK, 1, 0)
    total = tile_products(blocks, norms, piece[0], piece[1])
    partial_value = total.transpose(1, 0, 2).reshape(count_rhs, rows.shape[1])
    mine = summed_on_arrival(partial_value, OWN, 1)
    image = mine + noise_level * direction
    rr_sum, pq_sum, rq_sum, qq_sum = (
        one_axis_at_a_time(jnp.sum(residual * residual, axis=1), OWN_BLK),
        one_axis_at_a_time(jnp.sum(direction * image, axis=1), OWN_BLK),
        one_axis_at_a_time(jnp.sum(residual * image, axis=1), OWN_BLK),
        one_axis_at_a_time(jnp.sum(image * image, axis=1), OWN_BLK),
    )
    alpha = rr_sum / pq_sum
    residual_next = residual - alpha[:, None] * image
    new_sum = rr_sum - 2.0 * alpha * rq_sum + alpha * alpha * qq_sum
    solution_next = solution_field + alpha[:, None] * direction
    direction_next = residual_next + (new_sum / rr_sum)[:, None] * direction
    return (solution_next, residual_next, direction_next)


def solution(mesh):
    split = Mesh(mesh.devices.reshape(8, 4, 4, 2, 2), ("own_0", "own_1", "blk_0", "blk_1", "blk_2"))
    return jax.shard_map(
        local,
        mesh=split,
        in_specs=(P(None, OWN_BLK), P(None, OWN_BLK), P(None, OWN_BLK), P(None, OWN_BLK)),
        out_specs=(P(None, OWN_BLK), P(None, OWN_BLK), P(None, OWN_BLK)),
        check_vma=False,
    )
```

profile of v0, /device:TPU:1, one launch (start us, length us, event | category | flops | bytes accessed | tf_op | source)
XLA Modules:
  0.0 139.8 jit_solution(11596844076740842968)
XLA Ops:
  0.6 1.6 %broadcast_in_dim.11 = bf16[32,64,128]{2,1,0:T(8,128)(2,1)} broadcast(bf16[64,128]{1,0:T(8,128)(2,1)} %param.6), dimensions={1,2} | broadcast | bytes 540672 | tf_op jit(solution)/shard_map/broadcast_in_dim | solution.py:29
  2.3 16.6 %all-to-all-start = ((bf16[32,64,128]{2,1,0:T(8,128)(2,1)}), bf16[32,64,128]{2,1,0:T(8,128)(2,1)S(1)}, u32[]{:S(2)}, u32[]{:S(2)}) async-start(bf16[32,64,128]{2,1,0:T(8,128)(2,1)} %broadcast_in_dim.11), calls=%async_computation | async-start | bytes 1048576 | tf_op jit(solution)/shard_map/all_to_all | solution.py:28
  19.0 26.7 %all_gather.3 = bf16[97,2048]{1,0:T(8,128)(2,1)S(1)} all-gather(bf16[97,128]{1,0:T(8,128)(2,1)S(1)} %pad_maximum_fusion), channel_id=1, replica_groups=mesh['own_0'=8,'own_1'=4,'blk_0'=4,'blk_1'=2,'blk_2'=2] {'blk_0','blk_1'..., dimensions={1}, use_global_device_ids=true | all-gather | bytes 422144 | tf_op jit(solution)/shard_map/all_gather | solution.py:40
  45.8 0.3 copy.9
  46.2 0.3 reshape_reshape.6
  46.8 13.7 %while.10 = (s32[]{:T(128)}, f32[8,33,512]{2,1,0:T(8,128)S(1)}, f32[8,512]{1,0:T(8,128)S(1)}, f32[2048]{0:T(1024)S(1)}, bf16[8,64,512]{2,1,0:T(8,128)(2,1)S(1)},...) while((s32[]{:T(128)}, f32[8,33,512]{2,1,0:T(8,128)S(1)}, ...), condition=%wide.region_9.10_spmd, body=%wide.region_8.9_spmd.sunk | while | flops 209715200 | bytes 588889 | solution.py:73
  46.8 1.7 %fusion.21 = f32[8,33,512]{2,1,0:T(8,128)S(1)} fusion(f32[8,33,512]{2,1,0:T(8,128)S(1)} %get-tuple-element.150, s32[]{:T(128)} %get-tuple-element.149, bf16[33,2048]{1,0:T(8,128)(2,1)S(1)} %get-tuple-element.163, bf16[64,2048]{1,0:T(8,128)(2,1)S(1)} %get-tuple-element.162, f32[2048]{0:T(1024)S(1)} %get-tuple-element.160, f32[512]{0:T(512)S(1)} %bitcast.32, ...), kind=kOutput, calls=%fused_computation.3.clone.1 | convolution fusion | flops 209715200 | bytes 584704 | tf_op jit(solution)/shard_map/while/body/eval_jaxpr/dot_general | solution.py:69
  48.5 1.7 %fusion.21 = f32[8,33,512]{2,1,0:T(8,128)S(1)} fusion(f32[8,33,512]{2,1,0:T(8,128)S(1)} %get-tuple-element.150, s32[]{:T(128)} %get-tuple-element.149, bf16[33,2048]{1,0:T(8,128)(2,1)S(1)} %get-tuple-element.163, bf16[64,2048]{1,0:T(8,128)(2,1)S(1)} %get-tuple-element.162, f32[2048]{0:T(1024)S(1)} %get-tuple-element.160, f32[512]{0:T(512)S(1)} %bitcast.32, ...), kind=kOutput, calls=%fused_computation.3.clone.1 | convolution fusion | flops 209715200 | bytes 584704 | tf_op jit(solution)/shard_map/while/body/eval_jaxpr/dot_general | solution.py:69
  50.2 1.7 %fusion.21 = f32[8,33,512]{2,1,0:T(8,128)S(1)} fusion(f32[8,33,512]{2,1,0:T(8,128)S(1)} %get-tuple-element.150, s32[]{:T(128)} %get-tuple-element.149, bf16[33,2048]{1,0:T(8,128)(2,1)S(1)} %get-tuple-element.163, bf16[64,2048]{1,0:T(8,128)(2,1)S(1)} %get-tuple-element.162, f32[2048]{0:T(1024)S(1)} %get-tuple-element.160, f32[512]{0:T(512)S(1)} %bitcast.32, ...), kind=kOutput, calls=%fused_computation.3.clone.1 | convolution fusion | flops 209715200 | bytes 584704 | tf_op jit(solution)/shard_map/while/body/eval_jaxpr/dot_general | solution.py:69
  51.9 1.7 %fusion.21 = f32[8,33,512]{2,1,0:T(8,128)S(1)} fusion(f32[8,33,512]{2,1,0:T(8,128)S(1)} %get-tuple-element.150, s32[]{:T(128)} %get-tuple-element.149, bf16[33,2048]{1,0:T(8,128)(2,1)S(1)} %get-tuple-element.163, bf16[64,2048]{1,0:T(8,128)(2,1)S(1)} %get-tuple-element.162, f32[2048]{0:T(1024)S(1)} %get-tuple-element.160, f32[512]{0:T(512)S(1)} %bitcast.32, ...), kind=kOutput, calls=%fused_computation.3.clone.1 | convolution fusion | flops 209715200 | bytes 584704 | tf_op jit(solution)/shard_map/while/body/eval_jaxpr/dot_general | solution.py:69
  53.7 1.7 %fusion.21 = f32[8,33,512]{2,1,0:T(8,128)S(1)} fusion(f32[8,33,512]{2,1,0:T(8,128)S(1)} %get-tuple-element.150, s32[]{:T(128)} %get-tuple-element.149, bf16[33,2048]{1,0:T(8,128)(2,1)S(1)} %get-tuple-element.163, bf16[64,2048]{1,0:T(8,128)(2,1)S(1)} %get-tuple-element.162, f32[2048]{0:T(1024)S(1)} %get-tuple-element.160, f32[512]{0:T(512)S(1)} %bitcast.32, ...), kind=kOutput, calls=%fused_computation.3.clone.1 | convolution fusion | flops 209715200 | bytes 584704 | tf_op jit(solution)/shard_map/while/body/eval_jaxpr/dot_general | solution.py:69
  55.4 1.7 %fusion.21 = f32[8,33,512]{2,1,0:T(8,128)S(1)} fusion(f32[8,33,512]{2,1,0:T(8,128)S(1)} %get-tuple-element.150, s32[]{:T(128)} %get-tuple-element.149, bf16[33,2048]{1,0:T(8,128)(2,1)S(1)} %get-tuple-element.163, bf16[64,2048]{1,0:T(8,128)(2,1)S(1)} %get-tuple-element.162, f32[2048]{0:T(1024)S(1)} %get-tuple-element.160, f32[512]{0:T(512)S(1)} %bitcast.32, ...), kind=kOutput, calls=%fused_computation.3.clone.1 | convolution fusion | flops 209715200 | bytes 584704 | tf_op jit(solution)/shard_map/while/body/eval_jaxpr/dot_general | solution.py:69
  57.1 1.7 %fusion.21 = f32[8,33,512]{2,1,0:T(8,128)S(1)} fusion(f32[8,33,512]{2,1,0:T(8,128)S(1)} %get-tuple-element.150, s32[]{:T(128)} %get-tuple-element.149, bf16[33,2048]{1,0:T(8,128)(2,1)S(1)} %get-tuple-element.163, bf16[64,2048]{1,0:T(8,128)(2,1)S(1)} %get-tuple-element.162, f32[2048]{0:T(1024)S(1)} %get-tuple-element.160, f32[512]{0:T(512)S(1)} %bitcast.32, ...), kind=kOutput, calls=%fused_computation.3.clone.1 | convolution fusion | flops 209715200 | bytes 584704 | tf_op jit(solution)/shard_map/while/body/eval_jaxpr/dot_general | solution.py:69
  58.8 1.7 %fusion.21 = f32[8,33,512]{2,1,0:T(8,128)S(1)} fusion(f32[8,33,512]{2,1,0:T(8,128)S(1)} %get-tuple-element.150, s32[]{:T(128)} %get-tuple-element.149, bf16[33,2048]{1,0:T(8,128)(2,1)S(1)} %get-tuple-element.163, bf16[64,2048]{1,0:T(8,128)(2,1)S(1)} %get-tuple-element.162, f32[2048]{0:T(1024)S(1)} %get-tuple-element.160, f32[512]{0:T(512)S(1)} %bitcast.32, ...), kind=kOutput, calls=%fused_computation.3.clone.1 | convolution fusion | flops 209715200 | bytes 584704 | tf_op jit(solution)/shard_map/while/body/eval_jaxpr/dot_general | solution.py:69
  60.5 0.3 copy.11
  60.9 0.3 copy.12
  61.2 33.4 %all_to_all.10 = f32[32,33,128]{2,1,0:T(8,128)S(1)} all-to-all(f32[32,33,128]{2,1,0:T(8,128)S(1)} %copy.12), channel_id=1, replica_groups=mesh['own_0'=8,'own_1'=4,'blk_0'=4,'blk_1'=2,'blk_2'=2] {'own_0','own_1'}, dimensions={0} | all-to-all | bytes 1081344 | tf_op jit(solution)/shard_map/all_to_all | solution.py:51
  94.6 0.7 copy-done.1
  95.5 12.1 %all-reduce = (f32[33]{0:T(128)S(1)}, f32[33]{0:T(128)S(1)}, f32[33]{0:T(128)S(1)}, f32[33]{0:T(128)S(1)}) all-reduce(f32[33]{0:T(128)S(1)} %get-tuple-element.58, f32[33]{0:T(128)S(1)} %get-tuple-element.57, f32[33]{0:T(128)S(1)} %get-tuple-element.56, ...), channel_id=1, replica_groups=mesh['own_0'=8,'own_1'=4,'blk_0'=4,'blk_1'=2,'blk_2'=2] {'own_0'}, use_global_device_ids=true, to_apply=%region_1.0 | all-reduce | flops 132 | bytes 1056 | tf_op jit(solution)/shard_map/psum | solution.py:56
  107.6 9.4 %all-reduce.2 = (f32[33]{0:T(128)S(1)}, f32[33]{0:T(128)S(1)}, f32[33]{0:T(128)S(1)}, f32[33]{0:T(128)S(1)}) all-reduce(f32[33]{0:T(128)S(1)} %get-tuple-element.73, f32[33]{0:T(128)S(1)} %get-tuple-element.74, f32[33]{0:T(128)S(1)} %get-tuple-element.75, ...), channel_id=1, replica_groups=mesh['own_0'=8,'own_1'=4,'blk_0'=4,'blk_1'=2,'blk_2'=2] {'own_1'}, use_global_device_ids=true, to_apply=%region_2.3 | all-reduce | flops 132 | bytes 1056 | tf_op jit(solution)/shard_map/psum | solution.py:56
  117.0 6.3 %all-reduce.1 = (f32[33]{0:T(128)S(1)}, f32[33]{0:T(128)S(1)}, f32[33]{0:T(128)S(1)}, f32[33]{0:T(128)S(1)}) all-reduce(f32[33]{0:T(128)S(1)} %get-tuple-element.81, f32[33]{0:T(128)S(1)} %get-tuple-element.82, f32[33]{0:T(128)S(1)} %get-tuple-element.83, ...), channel_id=1, replica_groups=mesh['own_0'=8,'own_1'=4,'blk_0'=4,'blk_1'=2,'blk_2'=2] {'blk_0'}, use_global_device_ids=true, to_apply=%region_3.4 | all-reduce | flops 132 | bytes 1056 | tf_op jit(solution)/shard_map/psum | solution.py:56
  123.3 3.8 %all-reduce.4 = (f32[33]{0:T(128)S(1)}, f32[33]{0:T(128)S(1)}, f32[33]{0:T(128)S(1)}, f32[33]{0:T(128)S(1)}) all-reduce(f32[33]{0:T(128)S(1)} %get-tuple-element.77, f32[33]{0:T(128)S(1)} %get-tuple-element.78, f32[33]{0:T(128)S(1)} %get-tuple-element.79, ...), channel_id=1, replica_groups=mesh['own_0'=8,'own_1'=4,'blk_0'=4,'blk_1'=2,'blk_2'=2] {'blk_1'}, use_global_device_ids=true, to_apply=%region_4.5 | all-reduce | flops 132 | bytes 1056 | tf_op jit(solution)/shard_map/psum | solution.py:56
  127.1 12.0 %all-reduce.3 = (f32[33]{0:T(128)S(1)}, f32[33]{0:T(128)S(1)}, f32[33]{0:T(128)S(1)}, f32[33]{0:T(128)S(1)}) all-reduce(f32[33]{0:T(128)S(1)} %get-tuple-element.89, f32[33]{0:T(128)S(1)} %get-tuple-element.90, f32[33]{0:T(128)S(1)} %get-tuple-element.91, ...), channel_id=1, replica_groups=mesh['own_0'=8,'own_1'=4,'blk_0'=4,'blk_1'=2,'blk_2'=2] {'blk_2'}, use_global_device_ids=true, to_apply=%region_5.6 | all-reduce | flops 132 | bytes 1056 | tf_op jit(solution)/shard_map/psum | solution.py:56
  139.1 0.7 multiply_add_fusion
  (28 shorter events, 0.7 us)
Async XLA Ops:
  2.3 16.7 %copy-start = (f32[33,128]{1,0:T(8,128)S(1)}, f32[33,128]{1,0:T(8,128)}, u32[]{:S(2)}) copy-start(f32[33,128]{1,0:T(8,128)} %param.9) | copy-start | bytes 50692
  2.3 16.7 %copy-start.2 = (bf16[64,128]{1,0:T(8,128)(2,1)S(1)}, bf16[64,128]{1,0:T(8,128)(2,1)}, u32[]{:S(2)}) copy-start(bf16[64,128]{1,0:T(8,128)(2,1)} %param.6) | copy-start | bytes 49156
  2.3 43.5 %all-to-all-start = ((bf16[32,64,128]{2,1,0:T(8,128)(2,1)}), bf16[32,64,128]{2,1,0:T(8,128)(2,1)S(1)}, u32[]{:S(2)}, u32[]{:S(2)}) async-start(bf16[32,64,128]{2,1,0:T(8,128)(2,1)} %broadcast_in_dim.11), calls=%async_computation | async-start | bytes 1048576 | tf_op jit(solution)/shard_map/all_to_all | solution.py:28
  94.6 0.7 copy-start.1
  94.6 44.6 %copy-start.3 = (f32[33,128]{1,0:T(8,128)S(1)}, f32[33,128]{1,0:T(8,128)}, u32[]{:S(2)}) copy-start(f32[33,128]{1,0:T(8,128)} %param.7) | copy-start | bytes 50692
where the time goes:
time: 140 us
  blocking collectives  104 us (74%)
  starting transfers between devices  16.6 us (12%)
  matrix products  13.4 us (10%)
  local copies, waits for them, and re-layouts  3.89 us (3%)
    psum x5, blocking collectives, one_axis_at_a_time(): return functools.reduce(lax.psum, axes, shard)  43.7 us
    all_to_all x1, blocking collectives, summed_on_arrival(): lax.all_to_all(pieces, axis, split_axis=0, concat_axis=0, tiled=True)  33.4 us
    all_gather x1, blocking collectives, in_one_piece(): filled = lax.all_gather(both, axis, axis=dim, tiled=True)  26.7 us
    all_to_all x1, starting transfers between devices, copy_for_each(): lax.all_to_all(jnp.broadcast_to(shard[None], (peers, *shard.shape)), axis...  16.6 us
    dot_general x8, matrix products, single(): lax.dot_general(dirs, kern, (((1,), (1,)), ((), ())), preferred_element_t...  13.4 us
  transfers between devices with their start and end apart: 1, of which 0 were waited for; matrix products, arithmetic and copies ran while one was open for 0% of the time, Pallas kernels for 0%

commit v1 on v0

v1 whole, which is shorter than its diff:
```python
import functools
import math

import jax
import jax.numpy as jnp
from jax import lax
from jax.experimental import pallas as pl
from jax.experimental.pallas import tpu as pltpu
from jax.sharding import Mesh
from jax.sharding import PartitionSpec as P

f32 = jnp.float32
bf16 = jnp.bfloat16

ALL = ("y", "zh", "x", "zl", "c")
COLS = ("y", "zh")
ROWS = ("x", "zl", "c")
SUM_1 = ("y", "x")
SUM_2 = ("zh", "zl", "c")

amplitude = 1.0
decay_rate = 1.0 / 16.0
noise_level = 0.5
LOG2E = math.log2(math.e)
DEPTH = 128
LANES = 128
ROW_BLOCK = 512
COL_BLOCK = 4096
VMEM = 50 * 2**20


def copies(shard, axes):
    peers = lax.axis_size(axes)
    return lax.all_to_all(
        jnp.broadcast_to(shard[None], (peers, *shard.shape)), axes, 0, 0, tiled=True
    )


def norm_features(x, first):
    values = x.astype(f32)
    norms = jnp.sum(values * values, axis=0, keepdims=True) * (-decay_rate)
    high = norms.astype(bf16).astype(f32)
    middle = (norms - high).astype(bf16).astype(f32)
    low = norms - high - middle
    at = lax.broadcasted_iota(jnp.int32, x.shape, 0)
    ones = 3 - first
    out = jnp.where((at >= ones) & (at < ones + 3), 1.0, 0.0)
    for k, piece in enumerate((high, middle, low)):
        out = jnp.where(at == first + k, piece, out)
    return out.astype(bf16)


def product_kernel(rows_ref, cols_ref, out_ref, row_side, col_side, dirs):
    dim = rows_ref.shape[1]
    rhs = dirs.shape[0]

    def one_row_block(k, carry):
        x = rows_ref[k]
        here = pl.ds(pl.multiple_of(k * LANES, LANES), LANES)
        row_side[0:dim, here] = (x.astype(f32) * (2.0 * decay_rate)).astype(bf16)
        row_side[dim:DEPTH, here] = norm_features(x, 0)
        return carry

    def one_col_block(k, carry):
        both = cols_ref[k]
        x = both[0:dim]
        here = pl.ds(pl.multiple_of(k * LANES, LANES), LANES)
        col_side[here, :] = jnp.concatenate([x, norm_features(x, 3)], axis=0).T
        dirs[:, here] = both[dim : dim + rhs]
        return carry

    lax.fori_loop(0, rows_ref.shape[0], one_row_block, 0, unroll=4)
    lax.fori_loop(0, cols_ref.shape[0], one_col_block, 0, unroll=4)
    width = row_side.shape[1]
    depth = col_side.shape[0]

    def one_step(i, carry):
        here = pl.ds(pl.multiple_of(i * ROW_BLOCK, ROW_BLOCK), ROW_BLOCK)
        side = row_side[:, here]
        total = jnp.zeros((rhs, ROW_BLOCK), f32)
        for j in range(depth // COL_BLOCK):
            there = pl.ds(j * COL_BLOCK, COL_BLOCK)
            expo = jnp.dot(col_side[there, :], side, preferred_element_type=f32)
            kern = jnp.minimum((amplitude * jnp.exp2(expo * LOG2E)).astype(bf16), jnp.asarray(amplitude, bf16))
            total = total + jnp.dot(dirs[:, there], kern, preferred_element_type=f32)
        for k in range(ROW_BLOCK // LANES):
            out_ref[i * (ROW_BLOCK // LANES) + k] = total[:, k * LANES : (k + 1) * LANES]
        return carry

    lax.fori_loop(0, width // ROW_BLOCK, one_step, 0)


def partial_products(rows, cols):
    count_r, dim, _ = rows.shape
    count_c = cols.shape[0]
    rhs = cols.shape[1] - dim
    pairs = count_r * count_c * LANES * LANES
    return pl.pallas_call(
        product_kernel,
        out_shape=jax.ShapeDtypeStruct((count_r, rhs, LANES), f32),
        in_specs=[pl.BlockSpec(memory_space=pltpu.VMEM)] * 2,
        out_specs=pl.BlockSpec(memory_space=pltpu.VMEM),
        scratch_shapes=[
            pltpu.VMEM((DEPTH, count_r * LANES), bf16),
            pltpu.VMEM((count_c * LANES, DEPTH), bf16),
            pltpu.VMEM((rhs, count_c * LANES), bf16),
        ],
        compiler_params=pltpu.CompilerParams(vmem_limit_bytes=VMEM),
        cost_estimate=pl.CostEstimate(flops=2 * pairs * (DEPTH + rhs), bytes_accessed=2 * 2**20, transcendentals=pairs),
        name="products",
    )(rows, cols)


def local(points, solution_field, residual, direction):
    rhs = direction.shape[0]
    packed = jnp.concatenate([points, direction.astype(bf16)], axis=0)
    cols = copies(packed, COLS)
    rows = lax.all_gather(points[None], ("zl", "c"), axis=0, tiled=True)
    rows = lax.all_gather(rows, "x", axis=0, tiled=True)
    partial = partial_products(rows, cols)
    arrived = lax.all_to_all(partial, ROWS, 0, 0, tiled=True)
    image = arrived.sum(axis=0) + noise_level * direction
    sums = jnp.stack(
        [
            jnp.sum(residual * residual, axis=1),
            jnp.sum(direction * image, axis=1),
            jnp.sum(residual * image, axis=1),
            jnp.sum(image * image, axis=1),
        ]
    )
    sums = copies(sums, SUM_1).sum(axis=0)
    sums = copies(sums, SUM_2).sum(axis=0)
    rr_sum, pq_sum, rq_sum, qq_sum = sums[0], sums[1], sums[2], sums[3]
    alpha = rr_sum / pq_sum
    residual_next = residual - alpha[:, None] * image
    new_sum = rr_sum - 2.0 * alpha * rq_sum + alpha * alpha * qq_sum
    solution_next = solution_field + alpha[:, None] * direction
    direction_next = residual_next + (new_sum / rr_sum)[:, None] * direction
    return (solution_next, residual_next, direction_next)


def solution(mesh):
    split = Mesh(mesh.devices.reshape(8, 4, 4, 2, 2), ALL)
    spec = P(None, ALL)
    return jax.shard_map(
        local, mesh=split, in_specs=(spec,) * 4, out_specs=(spec,) * 3, check_vma=False
    )
```

time: 140 us -> 111 us (0.79)
  blocking collectives: 104 us -> 76.5 us
  matrix products: 13.4 us -> 0 us
  Pallas kernels: 0 us -> 8.88 us
  other arithmetic: 1.13 us -> 3.12 us
  waiting for transfers between devices: 0.01 us -> 1.84 us
    psum x5 -> x0, blocking collectives: 43.7 us -> none  [one_axis_at_a_time(): return functools.reduce(lax.psum, axes, shard)]
    all_to_all x1 -> x3, blocking collectives: 33.4 us -> 55.2 us  [the longest x2 39.4 us: copies(): lax.all_to_all(jnp.broadcast_to(shard[None], (peers, *shard.shape)), axes...]
    dot_general x8 -> x0, matrix products: 13.4 us -> none  [single(): lax.dot_general(dirs, kern, (((1,), (1,)), ((), ())), preferred_element_t...]
    pallas_call x0 -> x1, Pallas kernels: none -> 8.88 us  [partial_products(): pl.pallas_call(product_kernel, out_shape=jax.ShapeDtypeStruct((count_r, r...]
    all_gather x1 -> x2, blocking collectives: 26.7 us -> 21.3 us  [the longest x1 10.7 us: local(): rows = lax.all_gather(points[None], ('zl', 'c'), axis=0, tiled=True)]
    all_to_all x1, waiting for transfers between devices: 0.01 us -> 1.84 us  [copies(): lax.all_to_all(jnp.broadcast_to(shard[None], (peers, *shard.shape)), axes...]
    all_to_all x0 -> x2, other arithmetic: none -> 1.41 us  [copies(): lax.all_to_all(jnp.broadcast_to(shard[None], (peers, *shard.shape)), axes...]
  transfers between devices with their start and end apart: 1 -> 1, of which waited for: 0 -> 1; matrix products, arithmetic and copies ran while one was open for 0% -> 0% of each run, Pallas kernels for 0% -> 0%
where the time goes in v1:
time: 111 us
  blocking collectives  76.5 us (69%)
  starting transfers between devices  16.5 us (15%)
  Pallas kernels  8.88 us (8%)
  local copies, waits for them, and re-layouts  3.34 us (3%)
  other arithmetic  3.12 us (3%)
  waiting for transfers between devices  1.84 us (2%)
    all_to_all x2, blocking collectives, copies(): lax.all_to_all(jnp.broadcast_to(shard[None], (peers, *shard.shape)), axes...  39.4 us
    all_to_all x1, starting transfers between devices, copies(): lax.all_to_all(jnp.broadcast_to(shard[None], (peers, *shard.shape)), axes...  16.5 us
    all_to_all x1, blocking collectives, local(): arrived = lax.all_to_all(partial, ROWS, 0, 0, tiled=True)  15.8 us
    all_gather x1, blocking collectives, local(): rows = lax.all_gather(points[None], ('zl', 'c'), axis=0, tiled=True)  10.7 us
    all_gather x1, blocking collectives, local(): rows = lax.all_gather(rows, 'x', axis=0, tiled=True)  10.6 us
    pallas_call x1, Pallas kernels, partial_products(): pl.pallas_call(product_kernel, out_shape=jax.ShapeDtypeStruct((count_r, r...  8.88 us
  transfers between devices with their start and end apart: 1, of which 1 were waited for; matrix products, arithmetic and copies ran while one was open for 0% of the time, Pallas kernels for 0%

profile of v1, /device:TPU:1, one launch (start us, length us, event | category | flops | bytes accessed | tf_op | source)
XLA Modules:
  0.0 110.9 jit_solution(1398494935271724302)
XLA Ops:
  0.6 0.0 copy-start.2
  0.6 0.7 convert_element_type.3
  1.4 1.0 broadcast_in_dim.9
  2.4 16.5 %all-to-all-start = ((bf16[32,97,128]{2,1,0:T(8,128)(2,1)}), bf16[32,97,128]{2,1,0:T(8,128)(2,1)S(1)}, u32[]{:S(2)}, u32[]{:S(2)}) async-start(bf16[32,97,128]{2,1,0:T(8,128)(2,1)} %broadcast_in_dim.9), calls=%async_computation | async-start | bytes 1703936 | tf_op jit(solution)/shard_map/all_to_all | solution.py:34
  18.9 10.7 %all-gather = bf16[256,128]{1,0:T(8,128)(2,1)S(1)} all-gather(bf16[64,128]{1,0:T(8,128)(2,1)S(1)} %copy-done.2), channel_id=2, replica_groups=mesh['y'=8,'zh'=4,'x'=4,'zl'=2,'c'=2] {'zl','c'}, dimensions={0}, use_global_device_ids=true | all-gather | bytes 81920 | tf_op jit(solution)/shard_map/all_gather | solution.py:118
  29.6 10.6 %all_gather.7.rows_ref = bf16[16,64,128]{2,1,0:T(8,128)(2,1)S(1)} all-gather(bf16[4,64,128]{2,1,0:T(8,128)(2,1)S(1)} %bitcast.24), channel_id=1, replica_groups=mesh['y'=8,'zh'=4,'x'=4,'zl'=2,'c'=2] {'x'}, dimensions={0}, use_global_device_ids=true | all-gather | bytes 327680 | tf_op jit(solution)/shard_map/all_gather | solution.py:119
  40.2 1.8 %all-to-all-done.cols_ref = bf16[32,97,128]{2,1,0:T(8,128)(2,1)S(1)} async-done(((bf16[32,97,128]{2,1,0:T(8,128)(2,1)}), bf16[32,97,128]{2,1,0:T(8,128)(2,1)S(1)}, u32[]{:S(2)}, u32[]{:S(2)}) %all-to-all-start) | async-done | bytes 794656 | tf_op jit(solution)/shard_map/all_to_all | solution.py:34
  42.0 8.9 %products.1 = f32[16,33,128]{2,1,0:T(8,128)S(1)} custom-call(bf16[16,64,128]{2,1,0:T(8,128)(2,1)S(1)} %all_gather.7.rows_ref, bf16[32,97,128]{2,1,0:T(8,128)(2,1)S(1)} %all-to-all-done.cols_ref), custom_call_target="tpu_custom_call" | custom-call | flops 2701131776 | bytes 2097152 | tf_op jit(solution)/shard_map/products/pallas_call | solution.py:98
  50.9 15.8 %all_to_all.20 = f32[16,33,128]{2,1,0:T(8,128)S(1)} all-to-all(f32[16,33,128]{2,1,0:T(8,128)S(1)} %products.1), channel_id=1, replica_groups=mesh['y'=8,'zh'=4,'x'=4,'zl'=2,'c'=2] {'x','zl','c'}, dimensions={0} | all-to-all | bytes 540672 | tf_op jit(solution)/shard_map/all_to_all | solution.py:121
  66.7 0.7 copy-done
  67.4 0.0 copy-done.1
  67.5 0.1 multiply_reduce_fusion.2
  67.6 0.1 reshape.46
  67.8 24.4 %all_to_all.21 = f32[32,1,132]{2,1,0:T(1,128)S(1)} all-to-all(f32[32,1,132]{2,1,0:T(1,128)S(1)} %reshape.46), channel_id=1, replica_groups=mesh['y'=8,'zh'=4,'x'=4,'zl'=2,'c'=2] {'y','x'}, dimensions={0} | all-to-all | bytes 33792 | tf_op jit(solution)/shard_map/all_to_all | solution.py:34
  92.1 0.5 broadcast.7
  92.6 0.7 reduce
  93.4 0.1 reshape.47
  93.5 0.1 reshape.48
  93.6 15.0 %all_to_all.22 = f32[16,1,132]{2,1,0:T(1,128)S(1)} all-to-all(f32[16,1,132]{2,1,0:T(1,128)S(1)} %reshape.48), channel_id=1, replica_groups=mesh['y'=8,'zh'=4,'x'=4,'zl'=2,'c'=2] {'zh','zl','c'}, dimensions={0} | all-to-all | bytes 16896 | tf_op jit(solution)/shard_map/all_to_all | solution.py:34
  108.7 0.7 reduce.1
  109.4 0.1 reshape.49
  109.5 0.0 copy-start.3
  109.5 0.7 copy-done.3
  110.2 0.7 multiply_add_fusion
  (11 shorter events, 0.2 us)
Async XLA Ops:
  0.6 0.7 copy-start.2
  2.4 39.6 %all-to-all-start = ((bf16[32,97,128]{2,1,0:T(8,128)(2,1)}), bf16[32,97,128]{2,1,0:T(8,128)(2,1)S(1)}, u32[]{:S(2)}, u32[]{:S(2)}) async-start(bf16[32,97,128]{2,1,0:T(8,128)(2,1)} %broadcast_in_dim.9), calls=%async_computation | async-start | bytes 1703936 | tf_op jit(solution)/shard_map/all_to_all | solution.py:34
  66.7 0.7 copy-start
  66.7 0.7 copy-start.1
  109.5 0.7 copy-start.3

commit v2 on v1

v2 whole, which is shorter than its diff:
```python
import functools
import math

import jax
import jax.numpy as jnp
from jax import lax
from jax.experimental import pallas as pl
from jax.experimental.pallas import tpu as pltpu
from jax.sharding import Mesh
from jax.sharding import PartitionSpec as P

f32 = jnp.float32
bf16 = jnp.bfloat16

ALL = ("yh", "yl", "zh", "x", "zl", "c")
COLS = ("yh", "zh")
ROWS = ("yl", "x", "zl")
SUM_1 = ("yh", "yl", "x")
SUM_2 = ("zh", "zl", "c")

amplitude = 1.0
decay_rate = 1.0 / 16.0
noise_level = 0.5
LOG2E = math.log2(math.e)
DEPTH = 128
LANES = 128
ROW_BLOCK = 512
VMEM = 50 * 2**20
IN_VMEM = pl.BlockSpec(memory_space=pltpu.VMEM)


def kernel_call(body, out_shape, name, flops=10**6, scratch=()):
    outs = jax.tree.leaves(out_shape)
    return pl.pallas_call(
        body,
        out_shape=out_shape,
        out_specs=jax.tree.map(lambda _: IN_VMEM, out_shape),
        scratch_shapes=scratch,
        compiler_params=pltpu.CompilerParams(vmem_limit_bytes=VMEM),
        cost_estimate=pl.CostEstimate(
            flops=flops, bytes_accessed=sum(o.size * o.dtype.itemsize for o in outs), transcendentals=0
        ),
        name=name,
    )


def norm_features(x, first):
    values = x.astype(f32)
    norms = jnp.sum(values * values, axis=0, keepdims=True) * (-decay_rate)
    high = norms.astype(bf16).astype(f32)
    middle = (norms - high).astype(bf16).astype(f32)
    low = norms - high - middle
    at = lax.broadcasted_iota(jnp.int32, x.shape, 0)
    ones = 3 - first
    out = jnp.where((at >= ones) & (at < ones + 3), 1.0, 0.0)
    for k, piece in enumerate((high, middle, low)):
        out = jnp.where(at == first + k, piece, out)
    return out.astype(bf16)


def pack_kernel(points_ref, direction_ref, cols_ref, rows_ref):
    dim = points_ref.shape[0]
    both = jnp.concatenate([points_ref[...], direction_ref[...].astype(bf16)], axis=0)
    for k in range(cols_ref.shape[0]):
        cols_ref[k] = both
    for k in range(rows_ref.shape[0]):
        rows_ref[k] = both[0:dim]


def product_kernel(rows_ref, near_ref, far_ref, out_ref, row_side, col_side, dirs):
    dim = rows_ref.shape[1]
    rhs = dirs.shape[0]
    peers = near_ref.shape[0]

    def one_row_block(k, carry):
        x = rows_ref[k]
        here = pl.ds(pl.multiple_of(k * LANES, LANES), LANES)
        row_side[0:dim, here] = (x.astype(f32) * (2.0 * decay_rate)).astype(bf16)
        row_side[dim:DEPTH, here] = norm_features(x, 0)
        return carry

    def one_col_block(k, carry):
        for half, ref in enumerate((near_ref, far_ref)):
            both = ref[k]
            x = both[0:dim]
            here = pl.ds(pl.multiple_of((half * peers + k) * LANES, LANES), LANES)
            col_side[here, :] = jnp.concatenate([x, norm_features(x, 3)], axis=0).T
            dirs[:, here] = both[dim : dim + rhs]
        return carry

    lax.fori_loop(0, rows_ref.shape[0], one_row_block, 0, unroll=4)
    lax.fori_loop(0, peers, one_col_block, 0, unroll=2)

    def one_step(i, carry):
        here = pl.ds(pl.multiple_of(i * ROW_BLOCK, ROW_BLOCK), ROW_BLOCK)
        expo = jnp.dot(col_side[...], row_side[:, here], preferred_element_type=f32)
        kern = jnp.minimum((amplitude * jnp.exp2(expo * LOG2E)).astype(bf16), jnp.asarray(amplitude, bf16))
        total = jnp.dot(dirs[...], kern, preferred_element_type=f32)
        for k in range(ROW_BLOCK // LANES):
            out_ref[i * (ROW_BLOCK // LANES) + k] = total[:, k * LANES : (k + 1) * LANES]
        return carry

    lax.fori_loop(0, row_side.shape[1] // ROW_BLOCK, one_step, 0)


def to_lanes(values):
    square = jnp.broadcast_to(values, (values.shape[0], LANES))
    at = lax.broadcasted_iota(jnp.int32, square.shape, 0)
    lane = lax.broadcasted_iota(jnp.int32, square.shape, 1)
    return jnp.sum(jnp.where(at == lane, square, 0.0), axis=0, keepdims=True)


def sums_kernel(arrived_ref, direction_ref, residual_ref, image_ref, sums_ref):
    direction = direction_ref[...]
    residual = residual_ref[...]
    image = noise_level * direction
    total = arrived_ref[0]
    for k in range(1, arrived_ref.shape[0]):
        total = total + arrived_ref[k]
    image = total + image
    image_ref[...] = image
    products = (residual * residual, direction * image, residual * image, image * image)
    rows = [to_lanes(jnp.sum(v, axis=1, keepdims=True)) for v in products]
    sums = jnp.concatenate(rows, axis=0)
    for k in range(sums_ref.shape[0]):
        sums_ref[k] = sums


def middle_kernel(arrived_ref, sums_ref):
    sums = jnp.sum(arrived_ref[...], axis=0)
    for k in range(sums_ref.shape[0]):
        sums_ref[k] = sums


def to_rows(row, rhs):
    square = jnp.broadcast_to(row, (rhs, LANES))
    at = lax.broadcasted_iota(jnp.int32, square.shape, 0)
    lane = lax.broadcasted_iota(jnp.int32, square.shape, 1)
    return jnp.sum(jnp.where(at == lane, square, 0.0), axis=1, keepdims=True)


def last_kernel(arrived_ref, image_ref, solution_ref, residual_ref, direction_ref, s_ref, r_ref, d_ref):
    rhs = image_ref.shape[0]
    sums = jnp.sum(arrived_ref[...], axis=0)
    rr_sum, pq_sum, rq_sum, qq_sum = (to_rows(sums[k : k + 1], rhs) for k in range(4))
    alpha = rr_sum / pq_sum
    beta = (rr_sum - 2.0 * alpha * rq_sum + alpha * alpha * qq_sum) / rr_sum
    direction = direction_ref[...]
    residual_next = residual_ref[...] - alpha * image_ref[...]
    s_ref[...] = solution_ref[...] + alpha * direction
    r_ref[...] = residual_next
    d_ref[...] = residual_next + beta * direction


def local(points, solution_field, residual, direction):
    dim, width = points.shape
    rhs = direction.shape[0]
    peers_c, peers_r = lax.axis_size(COLS), lax.axis_size(ROWS)
    shape = jax.ShapeDtypeStruct
    cols, rows = kernel_call(
        pack_kernel,
        (shape((peers_c, dim + rhs, width), bf16), shape((peers_r, dim, width), bf16)),
        "pack",
    )(points, direction)
    cols = lax.all_to_all(cols, COLS, 0, 0, tiled=True)
    rows = lax.all_to_all(rows, ROWS, 0, 0, tiled=True)
    other = lax.ppermute(cols, "c", [(0, 1), (1, 0)])
    depth = 2 * peers_c * width
    pairs = depth * peers_r * width
    partial = kernel_call(
        product_kernel,
        shape((peers_r, rhs, width), f32),
        "products",
        flops=2 * pairs * (DEPTH + rhs),
        scratch=[
            pltpu.VMEM((DEPTH, peers_r * width), bf16),
            pltpu.VMEM((depth, DEPTH), bf16),
            pltpu.VMEM((rhs, depth), bf16),
        ],
    )(rows, cols, other)
    arrived = lax.all_to_all(partial, ROWS, 0, 0, tiled=True)
    image, sums = kernel_call(
        sums_kernel,
        (shape((rhs, width), f32), shape((lax.axis_size(SUM_1), 4, LANES), f32)),
        "sums",
    )(arrived, direction, residual)
    sums = lax.all_to_all(sums, SUM_1, 0, 0, tiled=True)
    sums = kernel_call(middle_kernel, shape((lax.axis_size(SUM_2), 4, LANES), f32), "middle")(sums)
    sums = lax.all_to_all(sums, SUM_2, 0, 0, tiled=True)
    out = shape((rhs, width), f32)
    return kernel_call(last_kernel, (out, out, out), "last")(
        sums, image, solution_field, residual, direction
    )


def solution(mesh):
    split = Mesh(mesh.devices.reshape(4, 2, 4, 4, 2, 2), ALL)
    spec = P(None, ALL)
    return jax.shard_map(
        local, mesh=split, in_specs=(spec,) * 4, out_specs=(spec,) * 3, check_vma=False
    )
```

time: 111 us -> 97.9 us (0.88)
  starting transfers between devices: 16.5 us -> 8.28 us
  blocking collectives: 76.5 us -> 73 us
  other arithmetic: 3.12 us -> 0 us
  local copies, waits for them, and re-layouts: 3.34 us -> 1.46 us
  Pallas kernels: 8.88 us -> 10.6 us
  waiting for transfers between devices: 1.84 us -> 3.26 us
    all_to_all x2 -> x3, blocking collectives: 39.4 us -> 61.5 us  [the longest x1 34.1 us: local(): cols = lax.all_to_all(cols, COLS, 0, 0, tiled=True)]
    all_gather x2 -> x0, blocking collectives: 21.3 us -> none  [the longest x1 10.7 us: local(): rows = lax.all_gather(points[None], ('zl', 'c'), axis=0, tiled=True)]
    all_to_all x1, starting transfers between devices: 16.5 us -> 4.84 us  [local(): rows = lax.all_to_all(rows, ROWS, 0, 0, tiled=True)]
    all_to_all x1, blocking collectives: 15.8 us -> 11.5 us  [local(): arrived = lax.all_to_all(partial, ROWS, 0, 0, tiled=True)]
    ppermute x0 -> x1, starting transfers between devices: none -> 3.44 us  [local(): other = lax.ppermute(cols, 'c', [(0, 1), (1, 0)])]
    pallas_call x1 -> x5, Pallas kernels: 8.88 us -> 10.6 us  [the longest x1 8.88 us: local(): kernel_call(product_kernel, shape((peers_r, rhs, width), f32), 'products'...]
    all_to_all x1, waiting for transfers between devices: 1.84 us -> 3.26 us  [local(): rows = lax.all_to_all(rows, ROWS, 0, 0, tiled=True)]
    all_to_all x2 -> x0, other arithmetic: 1.41 us -> none  [copies(): lax.all_to_all(jnp.broadcast_to(shard[None], (peers, *shard.shape)), axes...]
  transfers between devices with their start and end apart: 1 -> 2, of which waited for: 1 -> 1; matrix products, arithmetic and copies ran while one was open for 0% -> 0% of each run, Pallas kernels for 0% -> 0%
where the time goes in v2:
time: 97.9 us; the launch traced here: 97.3 us
  blocking collectives  73 us (75%)
  Pallas kernels  10.6 us (11%)
  starting transfers between devices  8.28 us (8%)
  waiting for transfers between devices  3.26 us (3%)
  local copies, waits for them, and re-layouts  1.46 us (1%)
    all_to_all x1, blocking collectives, local(): cols = lax.all_to_all(cols, COLS, 0, 0, tiled=True)  34.1 us
    all_to_all x1, blocking collectives, local(): sums = lax.all_to_all(sums, SUM_1, 0, 0, tiled=True)  13.9 us
    all_to_all x1, blocking collectives, local(): sums = lax.all_to_all(sums, SUM_2, 0, 0, tiled=True)  13.5 us
    all_to_all x1, blocking collectives, local(): arrived = lax.all_to_all(partial, ROWS, 0, 0, tiled=True)  11.5 us
    pallas_call x1, Pallas kernels, local(): kernel_call(product_kernel, shape((peers_r, rhs, width), f32), 'products'...  8.88 us
    all_to_all x1, starting transfers between devices, local(): rows = lax.all_to_all(rows, ROWS, 0, 0, tiled=True)  4.84 us
    ppermute x1, starting transfers between devices, local(): other = lax.ppermute(cols, 'c', [(0, 1), (1, 0)])  3.44 us
    all_to_all x1, waiting for transfers between devices, local(): rows = lax.all_to_all(rows, ROWS, 0, 0, tiled=True)  3.26 us
  transfers between devices with their start and end apart: 2, of which 1 were waited for; matrix products, arithmetic and copies ran while one was open for 0% of the time, Pallas kernels for 0%

profile of v2, /device:TPU:1, one launch (start us, length us, event | category | flops | bytes accessed | tf_op | source)
XLA Modules:
  0.0 97.3 jit_solution(11190337742761741277)
XLA Ops:
  0.6 0.0 copy-start
  0.6 0.7 copy-done
  1.4 0.0 copy-start.4
  1.4 0.7 copy-done.4
  2.1 0.8 pack.1
  2.9 34.1 %all_to_all.25.near_ref = bf16[16,97,128]{2,1,0:T(8,128)(2,1)S(1)} all-to-all(bf16[16,97,128]{2,1,0:T(8,128)(2,1)S(1)} %get-tuple-element.8), channel_id=1, replica_groups=mesh['yh'=4,'yl'=2,'zh'=4,'x'=4,'zl'=2,'c'=2] {'yh','zh'}, dimensions={0} | all-to-all | bytes 794624 | tf_op jit(solution)/shard_map/all_to_all | solution.py:165
  37.0 4.8 %all-to-all-start = ((bf16[16,64,128]{2,1,0:T(8,128)(2,1)}), bf16[16,64,128]{2,1,0:T(8,128)(2,1)S(1)}, u32[]{:S(2)}, u32[]{:S(2)}) async-start(bf16[16,64,128]{2,1,0:T(8,128)(2,1)} %get-tuple-element.7), calls=%async_computation | async-start | bytes 524288 | tf_op jit(solution)/shard_map/all_to_all | solution.py:166
  41.8 3.4 %collective-permute-start = (bf16[16,97,128]{2,1,0:T(8,128)(2,1)S(1)}, bf16[16,97,128]{2,1,0:T(8,128)(2,1)S(1)}, u32[]{:S(2)}, u32[]{:S(2)}) collective-permute-start(bf16[16,97,128]{2,1,0:T(8,128)(2,1)S(1)} %all_to_all.25.near_ref), channel_id=1, source_target_pairs={{0,1},{1,0},{2,3},{3,2},{4,5},{5,4},{6,7},{7,6},{8,9},{9,8},{10,11... | collective-permute-start | bytes 1191944 | tf_op jit(solution)/shard_map/ppermute | solution.py:167
  45.3 3.3 %all-to-all-done.rows_ref = bf16[16,64,128]{2,1,0:T(8,128)(2,1)S(1)} async-done(((bf16[16,64,128]{2,1,0:T(8,128)(2,1)}), bf16[16,64,128]{2,1,0:T(8,128)(2,1)S(1)}, u32[]{:S(2)}, u32[]{:S(2)}) %all-to-all-start) | async-done | bytes 262176 | tf_op jit(solution)/shard_map/all_to_all | solution.py:166
  48.5 0.0 collective-permute-done.far_ref
  48.5 8.9 %products.1 = f32[16,33,128]{2,1,0:T(8,128)S(1)} custom-call(bf16[16,64,128]{2,1,0:T(8,128)(2,1)S(1)} %all-to-all-done.rows_ref, bf16[16,97,128]{2,1,0:T(8,128)(2,1)S(1)} %all_to_all.25.near_ref, bf16[16,97,128]{2,1,0:T(8,128)(2,1)S(1)} %collective-permute-done.far_ref), custom_call_target="tpu_custom_call" | custom-call | flops 2701131776 | bytes 270336 | tf_op jit(solution)/shard_map/products/pallas_call | solution.py:170
  57.4 0.0 copy-start.1
  57.4 0.0 copy-start.2
  57.5 11.5 %all_to_all.26.arrived_ref = f32[16,33,128]{2,1,0:T(8,128)S(1)} all-to-all(f32[16,33,128]{2,1,0:T(8,128)S(1)} %products.1), channel_id=1, replica_groups=mesh['yh'=4,'yl'=2,'zh'=4,'x'=4,'zl'=2,'c'=2] {'yl','x','zl'}, dimensions={0} | all-to-all | bytes 540672 | tf_op jit(solution)/shard_map/all_to_all | solution.py:181
  69.0 0.0 copy-done.1
  69.0 0.0 copy-done.2
  69.0 0.1 sums.1
  69.1 13.9 %all_to_all.27.arrived_ref = f32[32,4,128]{2,1,0:T(4,128)S(1)} all-to-all(f32[32,4,128]{2,1,0:T(4,128)S(1)} %get-tuple-element.9), channel_id=1, replica_groups=mesh['yh'=4,'yl'=2,'zh'=4,'x'=4,'zl'=2,'c'=2] {'yh','yl','x'}, dimensions={0} | all-to-all | bytes 131072 | tf_op jit(solution)/shard_map/all_to_all | solution.py:187
  83.0 0.0 copy-start.3
  83.0 13.5 %all_to_all.28.arrived_ref = f32[16,4,128]{2,1,0:T(4,128)S(1)} all-to-all(f32[16,4,128]{2,1,0:T(4,128)S(1)} %middle.1), channel_id=1, replica_groups=mesh['yh'=4,'yl'=2,'zh'=4,'x'=4,'zl'=2,'c'=2] {'zh','zl','c'}, dimensions={0} | all-to-all | bytes 65536 | tf_op jit(solution)/shard_map/all_to_all | solution.py:189
  96.6 0.0 copy-done.3
  96.6 0.7 last.1
  (1 shorter events, 0.0 us)
Async XLA Ops:
  0.6 0.7 copy-start
  1.4 0.7 copy-start.4
  37.0 11.6 %all-to-all-start = ((bf16[16,64,128]{2,1,0:T(8,128)(2,1)}), bf16[16,64,128]{2,1,0:T(8,128)(2,1)S(1)}, u32[]{:S(2)}, u32[]{:S(2)}) async-start(bf16[16,64,128]{2,1,0:T(8,128)(2,1)} %get-tuple-element.7), calls=%async_computation | async-start | bytes 524288 | tf_op jit(solution)/shard_map/all_to_all | solution.py:166
  41.8 6.7 %collective-permute-start = (bf16[16,97,128]{2,1,0:T(8,128)(2,1)S(1)}, bf16[16,97,128]{2,1,0:T(8,128)(2,1)S(1)}, u32[]{:S(2)}, u32[]{:S(2)}) collective-permute-start(bf16[16,97,128]{2,1,0:T(8,128)(2,1)S(1)} %all_to_all.25.near_ref), channel_id=1, source_target_pairs={{0,1},{1,0},{2,3},{3,2},{4,5},{5,4},{6,7},{7,6},{8,9},{9,8},{10,11... | collective-permute-start | bytes 1191944 | tf_op jit(solution)/shard_map/ppermute | solution.py:167
  57.4 11.6 %copy-start.1 = (f32[33,128]{1,0:T(8,128)S(1)}, f32[33,128]{1,0:T(8,128)}, u32[]{:S(2)}) copy-start(f32[33,128]{1,0:T(8,128)} %direction_ref.5) | copy-start | bytes 50692
  57.4 11.6 %copy-start.2 = (f32[33,128]{1,0:T(8,128)S(1)}, f32[33,128]{1,0:T(8,128)}, u32[]{:S(2)}) copy-start(f32[33,128]{1,0:T(8,128)} %residual_ref.3) | copy-start | bytes 50692
  83.0 13.5 %copy-start.3 = (f32[33,128]{1,0:T(8,128)S(1)}, f32[33,128]{1,0:T(8,128)}, u32[]{:S(2)}) copy-start(f32[33,128]{1,0:T(8,128)} %solution_ref.1) | copy-start | bytes 50692

commit v3 on v2

--- a/solution.py
+++ b/solution.py
@@ -3,6 +3,7 @@
 
 import jax
 import jax.numpy as jnp
+import numpy as np
 from jax import lax
 from jax.experimental import pallas as pl
 from jax.experimental.pallas import tpu as pltpu
@@ -13,10 +14,10 @@
 bf16 = jnp.bfloat16
 
 ALL = ("yh", "yl", "zh", "x", "zl", "c")
-COLS = ("yh", "zh")
+SIZES = (4, 2, 4, 4, 2, 2)
 ROWS = ("yl", "x", "zl")
-SUM_1 = ("yh", "yl", "x")
-SUM_2 = ("zh", "zl", "c")
+SUM_1 = ("zh", "zl", "c")
+SUM_2 = ("yh", "yl", "x")
 
 amplitude = 1.0
 decay_rate = 1.0 / 16.0
@@ -24,16 +25,18 @@
 LOG2E = math.log2(math.e)
 DEPTH = 128
 LANES = 128
-ROW_BLOCK = 512
+ROW_BLOCK = 1024
 VMEM = 50 * 2**20
 IN_VMEM = pl.BlockSpec(memory_space=pltpu.VMEM)
 
 
-def kernel_call(body, out_shape, name, flops=10**6, scratch=()):
+def kernel_call(body, out_shape, name, flops=10**6, scratch=(), in_specs=None):
     outs = jax.tree.leaves(out_shape)
+    specs = {} if in_specs is None else {"in_specs": in_specs}
     return pl.pallas_call(
         body,
         out_shape=out_shape,
+        **specs,
         out_specs=jax.tree.map(lambda _: IN_VMEM, out_shape),
         scratch_shapes=scratch,
         compiler_params=pltpu.CompilerParams(vmem_limit_bytes=VMEM),
@@ -58,38 +61,42 @@
     return out.astype(bf16)
 
 
-def pack_kernel(points_ref, direction_ref, cols_ref, rows_ref):
-    dim = points_ref.shape[0]
-    both = jnp.concatenate([points_ref[...], direction_ref[...].astype(bf16)], axis=0)
-    for k in range(cols_ref.shape[0]):
-        cols_ref[k] = both
-    for k in range(rows_ref.shape[0]):
-        rows_ref[k] = both[0:dim]
-
-
-def product_kernel(rows_ref, near_ref, far_ref, out_ref, row_side, col_side, dirs):
-    dim = rows_ref.shape[1]
+def far_and_near():
+    at = np.arange(math.prod(SIZES)).reshape(SIZES)
+    far = at[..., 0].transpose(1, 3, 4, 0, 2).reshape(-1, SIZES[0] * SIZES[2])
+    near = at[..., 1].transpose(0, 2, 1, 3, 4).reshape(far.shape)
+    return np.concatenate([far, near]).tolist()
+
+
+def product_kernel(core_ref, mine_ref, other_ref, out_ref, row_side, col_side, dirs):
+    core = core_ref[0]
     rhs = dirs.shape[0]
-    peers = near_ref.shape[0]
-
-    def one_row_block(k, carry):
-        x = rows_ref[k]
-        here = pl.ds(pl.multiple_of(k * LANES, LANES), LANES)
-        row_side[0:dim, here] = (x.astype(f32) * (2.0 * decay_rate)).astype(bf16)
-        row_side[dim:DEPTH, here] = norm_features(x, 0)
-        return carry
-
-    def one_col_block(k, carry):
-        for half, ref in enumerate((near_ref, far_ref)):
-            both = ref[k]
-            x = both[0:dim]
-            here = pl.ds(pl.multiple_of((half * peers + k) * LANES, LANES), LANES)
-            col_side[here, :] = jnp.concatenate([x, norm_features(x, 3)], axis=0).T
-            dirs[:, here] = both[dim : dim + rhs]
-        return carry
-
-    lax.fori_loop(0, rows_ref.shape[0], one_row_block, 0, unroll=4)
-    lax.fori_loop(0, peers, one_col_block, 0, unroll=2)
+    dim = DEPTH // 2
+    peers = mine_ref.shape[0] // 2
+
+    def prepare(rows_ref, cols_ref, at):
+        def one_block(k, carry):
+            x = rows_ref[2 * k + at][0:dim]
+            here = pl.ds(pl.multiple_of(k * LANES, LANES), LANES)
+            row_side[0:dim, here] = (x.astype(f32) * (2.0 * decay_rate)).astype(bf16)
+            row_side[dim:DEPTH, here] = norm_features(x, 0)
+            for half in range(2):
+                both = cols_ref[2 * k + half]
+                x = both[0:dim]
+                here = pl.ds(pl.multiple_of((half * peers + k) * LANES, LANES), LANES)
+                col_side[here, :] = jnp.concatenate([x, norm_features(x, 3)], axis=0).T
+                dirs[:, here] = both[dim : dim + rhs]
+            return carry
+
+        lax.fori_loop(0, peers, one_block, 0, unroll=2)
+
+    @pl.when(core == 0)
+    def _():
+        prepare(other_ref, mine_ref, 0)
+
+    @pl.when(core == 1)
+    def _():
+        prepare(mine_ref, other_ref, 1)
 
     def one_step(i, carry):
         here = pl.ds(pl.multiple_of(i * ROW_BLOCK, ROW_BLOCK), ROW_BLOCK)
@@ -155,29 +162,29 @@
 def local(points, solution_field, residual, direction):
     dim, width = points.shape
     rhs = direction.shape[0]
-    peers_c, peers_r = lax.axis_size(COLS), lax.axis_size(ROWS)
     shape = jax.ShapeDtypeStruct
-    cols, rows = kernel_call(
-        pack_kernel,
-        (shape((peers_c, dim + rhs, width), bf16), shape((peers_r, dim, width), bf16)),
-        "pack",
-    )(points, direction)
-    cols = lax.all_to_all(cols, COLS, 0, 0, tiled=True)
-    rows = lax.all_to_all(rows, ROWS, 0, 0, tiled=True)
-    other = lax.ppermute(cols, "c", [(0, 1), (1, 0)])
-    depth = 2 * peers_c * width
-    pairs = depth * peers_r * width
+    both = jnp.concatenate([points, direction.astype(bf16)], axis=0)
+    groups = far_and_near()
+    peers = len(groups[0])
+    both = lax.all_gather(jnp.pad(both, ((0, -both.shape[0] % 8), (0, 0))), "c", axis=0, tiled=True)
+    both = both.reshape(2, -1, both.shape[1])
+    mine = jnp.broadcast_to(both[None], (peers, *both.shape)).reshape(-1, *both.shape[1:])
+    mine = lax.all_to_all(mine, ALL, 0, 0, axis_index_groups=groups, tiled=True)
+    other = lax.ppermute(mine, "c", [(0, 1), (1, 0)])
+    depth = 2 * peers * width
+    pairs = depth * peers * width
     partial = kernel_call(
         product_kernel,
-        shape((peers_r, rhs, width), f32),
+        shape((peers, rhs, width), f32),
         "products",
         flops=2 * pairs * (DEPTH + rhs),
         scratch=[
-            pltpu.VMEM((DEPTH, peers_r * width), bf16),
+            pltpu.VMEM((DEPTH, peers * width), bf16),
             pltpu.VMEM((depth, DEPTH), bf16),
             pltpu.VMEM((rhs, depth), bf16),
         ],
-    )(rows, cols, other)
+        in_specs=[pl.BlockSpec(memory_space=pltpu.SMEM), IN_VMEM, IN_VMEM],
+    )(lax.axis_index("c").reshape(1), mine, other)
     arrived = lax.all_to_all(partial, ROWS, 0, 0, tiled=True)
     image, sums = kernel_call(
         sums_kernel,
@@ -194,7 +201,7 @@
 
 
 def solution(mesh):
-    split = Mesh(mesh.devices.reshape(4, 2, 4, 4, 2, 2), ALL)
+    split = Mesh(mesh.devices.reshape(SIZES), ALL)
     spec = P(None, ALL)
     return jax.shard_map(
         local, mesh=split, in_specs=(spec,) * 4, out_specs=(spec,) * 3, check_vma=False

time: 97.9 us -> 91.7 us (0.937)
  blocking collectives: 73 us -> 58.5 us
  starting transfers between devices: 8.28 us -> 19.9 us
  local copies, waits for them, and re-layouts: 1.46 us -> 0.13 us
  waiting for transfers between devices: 3.26 us -> 1.98 us
  Pallas kernels: 10.6 us -> 9.41 us
    all_to_all x1, blocking collectives: 34.1 us -> 12.3 us  [local(): mine = lax.all_to_all(mine, ALL, 0, 0, axis_index_groups=groups, tiled=True)]
    ppermute x1, starting transfers between devices: 3.44 us -> 19.9 us  [local(): other = lax.ppermute(mine, 'c', [(0, 1), (1, 0)])]
    all_gather x0 -> x1, blocking collectives: none -> 8.38 us  [local(): lax.all_gather(jnp.pad(both, ((0, -both.shape[0] % 8), (0, 0))), 'c', axi...]
    all_to_all x1 -> x0, starting transfers between devices: 4.84 us -> none  [local(): rows = lax.all_to_all(rows, ROWS, 0, 0, tiled=True)]
    all_to_all x1 -> x0, waiting for transfers between devices: 3.26 us -> none  [local(): rows = lax.all_to_all(rows, ROWS, 0, 0, tiled=True)]
    ppermute x1, waiting for transfers between devices: 0.01 us -> 1.98 us  [local(): other = lax.ppermute(mine, 'c', [(0, 1), (1, 0)])]
    unnamed x10 -> x8, local copies, waits for them, and re-layouts: 1.46 us -> 0.02 us
    all_to_all x1, blocking collectives: 13.9 us -> 12.6 us  [local(): sums = lax.all_to_all(sums, SUM_1, 0, 0, tiled=True)]
  transfers between devices with their start and end apart: 2 -> 1, of which waited for: 1 -> 1; matrix products, arithmetic and copies ran while one was open for 0% -> 0% of each run, Pallas kernels for 0% -> 0%
where the time goes in v3:
time: 91.7 us; the launch traced here: 91.3 us
  blocking collectives  58.5 us (64%)
  starting transfers between devices  19.9 us (22%)
  Pallas kernels  9.41 us (10%)
  waiting for transfers between devices  1.98 us (2%)
    ppermute x1, starting transfers between devices, local(): other = lax.ppermute(mine, 'c', [(0, 1), (1, 0)])  19.9 us
    all_to_all x1, blocking collectives, local(): sums = lax.all_to_all(sums, SUM_2, 0, 0, tiled=True)  13.3 us
    all_to_all x1, blocking collectives, local(): sums = lax.all_to_all(sums, SUM_1, 0, 0, tiled=True)  12.6 us
    all_to_all x1, blocking collectives, local(): mine = lax.all_to_all(mine, ALL, 0, 0, axis_index_groups=groups, tiled=True)  12.3 us
    all_to_all x1, blocking collectives, local(): arrived = lax.all_to_all(partial, ROWS, 0, 0, tiled=True)  11.9 us
    pallas_call x1, Pallas kernels, local(): kernel_call(product_kernel, shape((peers, rhs, width), f32), 'products',...  8.51 us
    all_gather x1, blocking collectives, local(): lax.all_gather(jnp.pad(both, ((0, -both.shape[0] % 8), (0, 0))), 'c', axi...  8.38 us
    ppermute x1, waiting for transfers between devices, local(): other = lax.ppermute(mine, 'c', [(0, 1), (1, 0)])  1.98 us
  transfers between devices with their start and end apart: 1, of which 1 were waited for; matrix products, arithmetic and copies ran while one was open for 0% of the time, Pallas kernels for 0%

profile of v3, /device:TPU:1, one launch (start us, length us, event | category | flops | bytes accessed | tf_op | source)
XLA Modules:
  0.0 91.3 jit_solution(16134876701995719646)
XLA Ops:
  0.6 0.0 copy-start.3
  0.6 0.7 convert_element_type.5
  1.4 0.0 copy-done.3
  1.4 8.4 %all_gather.3 = bf16[208,128]{1,0:T(8,128)(2,1)S(1)} all-gather(bf16[104,128]{1,0:T(8,128)(2,1)S(1)} %fusion.2), channel_id=1, replica_groups=mesh['yh'=4,'yl'=2,'zh'=4,'x'=4,'zl'=2,'c'=2] {'c'}, dimensions={0}, use_global_device_ids=true | all-gather | bytes 79872 | tf_op jit(solution)/shard_map/all_gather | solution.py:169
  9.8 0.1 broadcast_in_dim.8
  9.9 12.3 %all_to_all.20.mine_ref = bf16[32,104,128]{2,1,0:T(8,128)(2,1)S(1)} all-to-all(bf16[32,104,128]{2,1,0:T(8,128)(2,1)S(1)} %bitcast.3), channel_id=1, replica_groups={{0,16,32,48,128,144,160,176,256,272,288,304,384,400,416,432},{2,18,34,5..., dimensions={0} | all-to-all | bytes 1703936 | tf_op jit(solution)/shard_map/all_to_all | solution.py:172
  22.2 19.9 %collective-permute-start = (bf16[32,104,128]{2,1,0:T(8,128)(2,1)S(1)}, bf16[32,104,128]{2,1,0:T(8,128)(2,1)S(1)}, u32[]{:S(2)}, u32[]{:S(2)}) collective-permute-start(bf16[32,104,128]{2,1,0:T(8,128)(2,1)S(1)} %all_to_all.20.mine_ref), channel_id=1, source_target_pairs={{0,1},{1,0},{2,3},{3,2},{4,5},{5,4},{6,7},{7,6},{8,9},{9,8},{10,11... | collective-permute-start | bytes 2555912 | tf_op jit(solution)/shard_map/ppermute | solution.py:173
  42.1 2.0 %collective-permute-done.other_ref = bf16[32,104,128]{2,1,0:T(8,128)(2,1)S(1)} collective-permute-done((bf16[32,104,128]{2,1,0:T(8,128)(2,1)S(1)}, bf16[32,104,128]{2,1,0:T(8,128)(2,1)S(1)}, u32[]{:S(2)}, u32[]{:S(2)}) %collective-permute-start) | collective-permute-done | bytes 852000 | tf_op jit(solution)/shard_map/ppermute | solution.py:173
  44.1 8.5 %products.1 = f32[16,33,128]{2,1,0:T(8,128)S(1)} custom-call(s32[1]{0:T(128)} %bitcast.core_ref, bf16[32,104,128]{2,1,0:T(8,128)(2,1)S(1)} %all_to_all.20.mine_ref, bf16[32,104,128]{2,1,0:T(8,128)(2,1)S(1)} %collective-permute-done.other_ref), custom_call_target="tpu_custom_call" | custom-call | flops 2701131776 | bytes 270336 | tf_op jit(solution)/shard_map/products/pallas_call | solution.py:176
  52.6 0.0 copy-start
  52.6 0.0 copy-start.1
  52.6 11.9 %all_to_all.21.arrived_ref = f32[16,33,128]{2,1,0:T(8,128)S(1)} all-to-all(f32[16,33,128]{2,1,0:T(8,128)S(1)} %products.1), channel_id=1, replica_groups=mesh['yh'=4,'yl'=2,'zh'=4,'x'=4,'zl'=2,'c'=2] {'yl','x','zl'}, dimensions={0} | all-to-all | bytes 540672 | tf_op jit(solution)/shard_map/all_to_all | solution.py:188
  64.5 0.0 copy-done
  64.5 0.0 copy-done.1
  64.5 0.1 sums.1
  64.6 12.6 %all_to_all.22.arrived_ref = f32[16,4,128]{2,1,0:T(4,128)S(1)} all-to-all(f32[16,4,128]{2,1,0:T(4,128)S(1)} %get-tuple-element.5), channel_id=1, replica_groups=mesh['yh'=4,'yl'=2,'zh'=4,'x'=4,'zl'=2,'c'=2] {'zh','zl','c'}, dimensions={0} | all-to-all | bytes 65536 | tf_op jit(solution)/shard_map/all_to_all | solution.py:194
  77.2 0.0 copy-start.2
  77.3 13.3 %all_to_all.23.arrived_ref = f32[32,4,128]{2,1,0:T(4,128)S(1)} all-to-all(f32[32,4,128]{2,1,0:T(4,128)S(1)} %middle.1), channel_id=1, replica_groups=mesh['yh'=4,'yl'=2,'zh'=4,'x'=4,'zl'=2,'c'=2] {'yh','yl','x'}, dimensions={0} | all-to-all | bytes 131072 | tf_op jit(solution)/shard_map/all_to_all | solution.py:196
  90.5 0.0 copy-done.2
  90.5 0.7 last.1
  (2 shorter events, 0.0 us)
Async XLA Ops:
  0.6 0.7 copy-start.3
  22.2 21.8 %collective-permute-start = (bf16[32,104,128]{2,1,0:T(8,128)(2,1)S(1)}, bf16[32,104,128]{2,1,0:T(8,128)(2,1)S(1)}, u32[]{:S(2)}, u32[]{:S(2)}) collective-permute-start(bf16[32,104,128]{2,1,0:T(8,128)(2,1)S(1)} %all_to_all.20.mine_ref), channel_id=1, source_target_pairs={{0,1},{1,0},{2,3},{3,2},{4,5},{5,4},{6,7},{7,6},{8,9},{9,8},{10,11... | collective-permute-start | bytes 2555912 | tf_op jit(solution)/shard_map/ppermute | solution.py:173
  52.6 12.0 %copy-start = (f32[33,128]{1,0:T(8,128)S(1)}, f32[33,128]{1,0:T(8,128)}, u32[]{:S(2)}) copy-start(f32[33,128]{1,0:T(8,128)} %direction_ref.3) | copy-start | bytes 50692
  52.6 11.9 %copy-start.1 = (f32[33,128]{1,0:T(8,128)S(1)}, f32[33,128]{1,0:T(8,128)}, u32[]{:S(2)}) copy-start(f32[33,128]{1,0:T(8,128)} %residual_ref.3) | copy-start | bytes 50692
  77.2 13.3 %copy-start.2 = (f32[33,128]{1,0:T(8,128)S(1)}, f32[33,128]{1,0:T(8,128)}, u32[]{:S(2)}) copy-start(f32[33,128]{1,0:T(8,128)} %solution_ref.1) | copy-start | bytes 50692

commit v4 on v3

--- a/solution.py
+++ b/solution.py
@@ -26,6 +26,7 @@
 DEPTH = 128
 LANES = 128
 ROW_BLOCK = 1024
+COL_CHUNKS = 4
 VMEM = 50 * 2**20
 IN_VMEM = pl.BlockSpec(memory_space=pltpu.VMEM)
 
@@ -69,52 +70,67 @@
 
 
 def product_kernel(core_ref, mine_ref, other_ref, out_ref, row_side, col_side, dirs):
-    core = core_ref[0]
+    first = core_ref[0] == 0
     rhs = dirs.shape[0]
     dim = DEPTH // 2
-    peers = mine_ref.shape[0] // 2
-
-    def prepare(rows_ref, cols_ref, at):
-        def one_block(k, carry):
-            x = rows_ref[2 * k + at][0:dim]
-            here = pl.ds(pl.multiple_of(k * LANES, LANES), LANES)
-            row_side[0:dim, here] = (x.astype(f32) * (2.0 * decay_rate)).astype(bf16)
-            row_side[dim:DEPTH, here] = norm_features(x, 0)
-            for half in range(2):
-                both = cols_ref[2 * k + half]
-                x = both[0:dim]
-                here = pl.ds(pl.multiple_of((half * peers + k) * LANES, LANES), LANES)
-                col_side[here, :] = jnp.concatenate([x, norm_features(x, 3)], axis=0).T
-                dirs[:, here] = both[dim : dim + rhs]
-            return carry
-
-        lax.fori_loop(0, peers, one_block, 0, unroll=2)
-
-    @pl.when(core == 0)
-    def _():
-        prepare(other_ref, mine_ref, 0)
-
-    @pl.when(core == 1)
-    def _():
-        prepare(mine_ref, other_ref, 1)
+    count_r = row_side.shape[1] // LANES
+    count_c = col_side.shape[0] // LANES
+    per_step = ROW_BLOCK // LANES
+
+    def prepare_rows(k):
+        x = jnp.where(first, other_ref[2 * k][0:dim], mine_ref[2 * k + 1][0:dim])
+        here = slice(k * LANES, (k + 1) * LANES)
+        row_side[0:dim, here] = (x.astype(f32) * (2.0 * decay_rate)).astype(bf16)
+        row_side[dim:DEPTH, here] = norm_features(x, 0)
+
+    def prepare_cols(k):
+        both = jnp.where(first, mine_ref[k], other_ref[k])
+        x = both[0:dim]
+        here = slice(k * LANES, (k + 1) * LANES)
+        col_side[here, :] = jnp.concatenate([x, norm_features(x, 3)], axis=0).T
+        dirs[:, here] = both[dim : dim + rhs]
+
+    def products(rows, cols):
+        expo = jnp.dot(col_side[cols, :], row_side[:, rows], preferred_element_type=f32)
+        kern = jnp.minimum((amplitude * jnp.exp2(expo * LOG2E)).astype(bf16), jnp.asarray(amplitude, bf16))
+        return jnp.dot(dirs[:, cols], kern, preferred_element_type=f32)
+
+    def store(i, total):
+        for k in range(per_step):
+            out_ref[i * per_step + k] = total[:, k * LANES : (k + 1) * LANES]
+
+    chunk = count_c // COL_CHUNKS
+    later = list(range(per_step, count_r))
+    share = -(-len(later) // COL_CHUNKS)
+    for k in range(per_step):
+        prepare_rows(k)
+    for k in range(chunk):
+        prepare_cols(k)
+    total = jnp.zeros((rhs, ROW_BLOCK), f32)
+    for q in range(COL_CHUNKS):
+        if q + 1 < COL_CHUNKS:
+            for k in range((q + 1) * chunk, (q + 2) * chunk):
+                prepare_cols(k)
+        for k in later[q * share : (q + 1) * share]:
+            prepare_rows(k)
+        cols = slice(q * chunk * LANES, (q + 1) * chunk * LANES)
+        total = total + products(slice(0, ROW_BLOCK), cols)
+    store(0, total)
 
     def one_step(i, carry):
         here = pl.ds(pl.multiple_of(i * ROW_BLOCK, ROW_BLOCK), ROW_BLOCK)
-        expo = jnp.dot(col_side[...], row_side[:, here], preferred_element_type=f32)
-        kern = jnp.minimum((amplitude * jnp.exp2(expo * LOG2E)).astype(bf16), jnp.asarray(amplitude, bf16))
-        total = jnp.dot(dirs[...], kern, preferred_element_type=f32)
-        for k in range(ROW_BLOCK // LANES):
-            out_ref[i * (ROW_BLOCK // LANES) + k] = total[:, k * LANES : (k + 1) * LANES]
+        store(i, products(here, slice(0, count_c * LANES)))
         return carry
 
-    lax.fori_loop(0, row_side.shape[1] // ROW_BLOCK, one_step, 0)
-
-
-def to_lanes(values):
-    square = jnp.broadcast_to(values, (values.shape[0], LANES))
-    at = lax.broadcasted_iota(jnp.int32, square.shape, 0)
-    lane = lax.broadcasted_iota(jnp.int32, square.shape, 1)
-    return jnp.sum(jnp.where(at == lane, square, 0.0), axis=0, keepdims=True)
+    lax.fori_loop(1, count_r // per_step, one_step, 0)
+
+
+def to_lanes(first, second):
+    shape = (first.shape[0], LANES)
+    at = lax.broadcasted_iota(jnp.int32, shape, 0)
+    lane = lax.broadcasted_iota(jnp.int32, shape, 1)
+    square = jnp.where(at == lane, first, jnp.where(at + LANES // 2 == lane, second, 0.0))
+    return jnp.sum(square, axis=0, keepdims=True)
 
 
 def sums_kernel(arrived_ref, direction_ref, residual_ref, image_ref, sums_ref):
@@ -127,8 +143,8 @@
     image = total + image
     image_ref[...] = image
     products = (residual * residual, direction * image, residual * image, image * image)
-    rows = [to_lanes(jnp.sum(v, axis=1, keepdims=True)) for v in products]
-    sums = jnp.concatenate(rows, axis=0)
+    rr_sum, pq_sum, rq_sum, qq_sum = (jnp.sum(v, axis=1, keepdims=True) for v in products)
+    sums = jnp.concatenate([to_lanes(rr_sum, pq_sum), to_lanes(rq_sum, qq_sum)], axis=0)
     for k in range(sums_ref.shape[0]):
         sums_ref[k] = sums
 
@@ -143,13 +159,17 @@
     square = jnp.broadcast_to(row, (rhs, LANES))
     at = lax.broadcasted_iota(jnp.int32, square.shape, 0)
     lane = lax.broadcasted_iota(jnp.int32, square.shape, 1)
-    return jnp.sum(jnp.where(at == lane, square, 0.0), axis=1, keepdims=True)
+    return (
+        jnp.sum(jnp.where(at == lane, square, 0.0), axis=1, keepdims=True),
+        jnp.sum(jnp.where(at + LANES // 2 == lane, square, 0.0), axis=1, keepdims=True),
+    )
 
 
 def last_kernel(arrived_ref, image_ref, solution_ref, residual_ref, direction_ref, s_ref, r_ref, d_ref):
     rhs = image_ref.shape[0]
     sums = jnp.sum(arrived_ref[...], axis=0)
-    rr_sum, pq_sum, rq_sum, qq_sum = (to_rows(sums[k : k + 1], rhs) for k in range(4))
+    rr_sum, pq_sum = to_rows(sums[0:1], rhs)
+    rq_sum, qq_sum = to_rows(sums[1:2], rhs)
     alpha = rr_sum / pq_sum
     beta = (rr_sum - 2.0 * alpha * rq_sum + alpha * alpha * qq_sum) / rr_sum
     direction = direction_ref[...]
@@ -188,11 +208,11 @@
     arrived = lax.all_to_all(partial, ROWS, 0, 0, tiled=True)
     image, sums = kernel_call(
         sums_kernel,
-        (shape((rhs, width), f32), shape((lax.axis_size(SUM_1), 4, LANES), f32)),
+        (shape((rhs, width), f32), shape((lax.axis_size(SUM_1), 2, LANES), f32)),
         "sums",
     )(arrived, direction, residual)
     sums = lax.all_to_all(sums, SUM_1, 0, 0, tiled=True)
-    sums = kernel_call(middle_kernel, shape((lax.axis_size(SUM_2), 4, LANES), f32), "middle")(sums)
+    sums = kernel_call(middle_kernel, shape((lax.axis_size(SUM_2), 2, LANES), f32), "middle")(sums)
     sums = lax.all_to_all(sums, SUM_2, 0, 0, tiled=True)
     out = shape((rhs, width), f32)
     return kernel_call(last_kernel, (out, out, out), "last")(

time: 91.7 us -> 90.8 us (level)
  no operation moved by 1% of the time
where the time goes in v4:
time: 90.8 us; the launch traced here: 90.4 us
  blocking collectives  58.2 us (64%)
  starting transfers between devices  19.9 us (22%)
  Pallas kernels  8.84 us (10%)
  waiting for transfers between devices  1.98 us (2%)
    ppermute x1, starting transfers between devices, local(): other = lax.ppermute(mine, 'c', [(0, 1), (1, 0)])  19.9 us
    all_to_all x1, blocking collectives, local(): sums = lax.all_to_all(sums, SUM_2, 0, 0, tiled=True)  13.1 us
    all_to_all x1, blocking collectives, local(): sums = lax.all_to_all(sums, SUM_1, 0, 0, tiled=True)  12.5 us
    all_to_all x1, blocking collectives, local(): mine = lax.all_to_all(mine, ALL, 0, 0, axis_index_groups=groups, tiled=True)  12.3 us
    all_to_all x1, blocking collectives, local(): arrived = lax.all_to_all(partial, ROWS, 0, 0, tiled=True)  11.8 us
    all_gather x1, blocking collectives, local(): lax.all_gather(jnp.pad(both, ((0, -both.shape[0] % 8), (0, 0))), 'c', axi...  8.38 us
    pallas_call x1, Pallas kernels, local(): kernel_call(product_kernel, shape((peers, rhs, width), f32), 'products',...  7.95 us
    ppermute x1, waiting for transfers between devices, local(): other = lax.ppermute(mine, 'c', [(0, 1), (1, 0)])  1.98 us
  transfers between devices with their start and end apart: 1, of which 1 were waited for; matrix products, arithmetic and copies ran while one was open for 0% of the time, Pallas kernels for 0%

profile of v4, /device:TPU:1, one launch (start us, length us, event | category | flops | bytes accessed | tf_op | source)
XLA Modules:
  0.0 90.4 jit_solution(14088548041769474587)
XLA Ops:
  0.6 0.0 copy-start.3
  0.6 0.7 convert_element_type.5
  1.4 0.0 copy-done.3
  1.4 8.4 %all_gather.3 = bf16[208,128]{1,0:T(8,128)(2,1)S(1)} all-gather(bf16[104,128]{1,0:T(8,128)(2,1)S(1)} %fusion.2), channel_id=1, replica_groups=mesh['yh'=4,'yl'=2,'zh'=4,'x'=4,'zl'=2,'c'=2] {'c'}, dimensions={0}, use_global_device_ids=true | all-gather | bytes 79872 | tf_op jit(solution)/shard_map/all_gather | solution.py:189
  9.8 0.1 broadcast_in_dim.8
  9.9 12.3 %all_to_all.20.mine_ref = bf16[32,104,128]{2,1,0:T(8,128)(2,1)S(1)} all-to-all(bf16[32,104,128]{2,1,0:T(8,128)(2,1)S(1)} %bitcast.3), channel_id=1, replica_groups={{0,16,32,48,128,144,160,176,256,272,288,304,384,400,416,432},{2,18,34,5..., dimensions={0} | all-to-all | bytes 1703936 | tf_op jit(solution)/shard_map/all_to_all | solution.py:192
  22.2 19.9 %collective-permute-start = (bf16[32,104,128]{2,1,0:T(8,128)(2,1)S(1)}, bf16[32,104,128]{2,1,0:T(8,128)(2,1)S(1)}, u32[]{:S(2)}, u32[]{:S(2)}) collective-permute-start(bf16[32,104,128]{2,1,0:T(8,128)(2,1)S(1)} %all_to_all.20.mine_ref), channel_id=1, source_target_pairs={{0,1},{1,0},{2,3},{3,2},{4,5},{5,4},{6,7},{7,6},{8,9},{9,8},{10,11... | collective-permute-start | bytes 2555912 | tf_op jit(solution)/shard_map/ppermute | solution.py:193
  42.1 2.0 %collective-permute-done.other_ref = bf16[32,104,128]{2,1,0:T(8,128)(2,1)S(1)} collective-permute-done((bf16[32,104,128]{2,1,0:T(8,128)(2,1)S(1)}, bf16[32,104,128]{2,1,0:T(8,128)(2,1)S(1)}, u32[]{:S(2)}, u32[]{:S(2)}) %collective-permute-start) | collective-permute-done | bytes 852000 | tf_op jit(solution)/shard_map/ppermute | solution.py:193
  44.1 7.9 %products.1 = f32[16,33,128]{2,1,0:T(8,128)S(1)} custom-call(s32[1]{0:T(128)} %bitcast.core_ref, bf16[32,104,128]{2,1,0:T(8,128)(2,1)S(1)} %all_to_all.20.mine_ref, bf16[32,104,128]{2,1,0:T(8,128)(2,1)S(1)} %collective-permute-done.other_ref), custom_call_target="tpu_custom_call" | custom-call | flops 2701131776 | bytes 270336 | tf_op jit(solution)/shard_map/products/pallas_call | solution.py:196
  52.0 0.0 copy-start
  52.0 0.0 copy-start.1
  52.0 11.8 %all_to_all.21.arrived_ref = f32[16,33,128]{2,1,0:T(8,128)S(1)} all-to-all(f32[16,33,128]{2,1,0:T(8,128)S(1)} %products.1), channel_id=1, replica_groups=mesh['yh'=4,'yl'=2,'zh'=4,'x'=4,'zl'=2,'c'=2] {'yl','x','zl'}, dimensions={0} | all-to-all | bytes 540672 | tf_op jit(solution)/shard_map/all_to_all | solution.py:208
  63.8 0.0 copy-done
  63.8 0.0 copy-done.1
  63.8 0.1 sums.1
  64.0 12.5 %all_to_all.22.arrived_ref = f32[16,2,128]{2,1,0:T(2,128)S(1)} all-to-all(f32[16,2,128]{2,1,0:T(2,128)S(1)} %get-tuple-element.5), channel_id=1, replica_groups=mesh['yh'=4,'yl'=2,'zh'=4,'x'=4,'zl'=2,'c'=2] {'zh','zl','c'}, dimensions={0} | all-to-all | bytes 32768 | tf_op jit(solution)/shard_map/all_to_all | solution.py:214
  76.5 0.0 copy-start.2
  76.5 13.1 %all_to_all.23.arrived_ref = f32[32,2,128]{2,1,0:T(2,128)S(1)} all-to-all(f32[32,2,128]{2,1,0:T(2,128)S(1)} %middle.1), channel_id=1, replica_groups=mesh['yh'=4,'yl'=2,'zh'=4,'x'=4,'zl'=2,'c'=2] {'yh','yl','x'}, dimensions={0} | all-to-all | bytes 65536 | tf_op jit(solution)/shard_map/all_to_all | solution.py:216
  89.7 0.0 copy-done.2
  89.7 0.7 last.1
  (2 shorter events, 0.0 us)
Async XLA Ops:
  0.6 0.7 copy-start.3
  22.2 21.8 %collective-permute-start = (bf16[32,104,128]{2,1,0:T(8,128)(2,1)S(1)}, bf16[32,104,128]{2,1,0:T(8,128)(2,1)S(1)}, u32[]{:S(2)}, u32[]{:S(2)}) collective-permute-start(bf16[32,104,128]{2,1,0:T(8,128)(2,1)S(1)} %all_to_all.20.mine_ref), channel_id=1, source_target_pairs={{0,1},{1,0},{2,3},{3,2},{4,5},{5,4},{6,7},{7,6},{8,9},{9,8},{10,11... | collective-permute-start | bytes 2555912 | tf_op jit(solution)/shard_map/ppermute | solution.py:193
  52.0 11.8 %copy-start = (f32[33,128]{1,0:T(8,128)S(1)}, f32[33,128]{1,0:T(8,128)}, u32[]{:S(2)}) copy-start(f32[33,128]{1,0:T(8,128)} %direction_ref.3) | copy-start | bytes 50692
  52.0 11.8 %copy-start.1 = (f32[33,128]{1,0:T(8,128)S(1)}, f32[33,128]{1,0:T(8,128)}, u32[]{:S(2)}) copy-start(f32[33,128]{1,0:T(8,128)} %residual_ref.3) | copy-start | bytes 50692
  76.5 13.2 %copy-start.2 = (f32[33,128]{1,0:T(8,128)S(1)}, f32[33,128]{1,0:T(8,128)}, u32[]{:S(2)}) copy-start(f32[33,128]{1,0:T(8,128)} %solution_ref.1) | copy-start | bytes 50692

commit v5 on v4

--- a/solution.py
+++ b/solution.py
@@ -69,8 +69,9 @@
     return np.concatenate([far, near]).tolist()
 
 
-def product_kernel(core_ref, mine_ref, other_ref, out_ref, row_side, col_side, dirs):
-    first = core_ref[0] == 0
+def product_kernel(place_ref, mine_ref, other_ref, out_ref, own_ref, row_side, col_side, dirs, parts):
+    first = lax.rem(place_ref[0], 2) == 0
+    me = lax.div(place_ref[0], 2)
     rhs = dirs.shape[0]
     dim = DEPTH // 2
     count_r = row_side.shape[1] // LANES
@@ -97,7 +98,9 @@
 
     def store(i, total):
         for k in range(per_step):
-            out_ref[i * per_step + k] = total[:, k * LANES : (k + 1) * LANES]
+            part = total[:, k * LANES : (k + 1) * LANES]
+            out_ref[i * per_step + k] = part.astype(bf16)
+            parts[i * per_step + k] = part
 
     chunk = count_c // COL_CHUNKS
     later = list(range(per_step, count_r))
@@ -123,6 +126,8 @@
         return carry
 
     lax.fori_loop(1, count_r // per_step, one_step, 0)
+    own_ref[...] = parts[me]
+    out_ref[me] = jnp.zeros((rhs, LANES), bf16)
 
 
 def to_lanes(first, second):
@@ -133,13 +138,13 @@
     return jnp.sum(square, axis=0, keepdims=True)
 
 
-def sums_kernel(arrived_ref, direction_ref, residual_ref, image_ref, sums_ref):
+def sums_kernel(arrived_ref, own_ref, direction_ref, residual_ref, image_ref, sums_ref):
     direction = direction_ref[...]
     residual = residual_ref[...]
     image = noise_level * direction
-    total = arrived_ref[0]
-    for k in range(1, arrived_ref.shape[0]):
-        total = total + arrived_ref[k]
+    total = own_ref[...]
+    for k in range(arrived_ref.shape[0]):
+        total = total + arrived_ref[k].astype(f32)
     image = total + image
     image_ref[...] = image
     products = (residual * residual, direction * image, residual * image, image * image)
@@ -193,24 +198,26 @@
     other = lax.ppermute(mine, "c", [(0, 1), (1, 0)])
     depth = 2 * peers * width
     pairs = depth * peers * width
-    partial = kernel_call(
+    place = (2 * lax.axis_index(ROWS) + lax.axis_index("c")).reshape(1)
+    partial, own = kernel_call(
         product_kernel,
-        shape((peers, rhs, width), f32),
+        (shape((peers, rhs, width), bf16), shape((rhs, width), f32)),
         "products",
         flops=2 * pairs * (DEPTH + rhs),
         scratch=[
             pltpu.VMEM((DEPTH, peers * width), bf16),
             pltpu.VMEM((depth, DEPTH), bf16),
             pltpu.VMEM((rhs, depth), bf16),
+            pltpu.VMEM((peers, rhs, width), f32),
         ],
         in_specs=[pl.BlockSpec(memory_space=pltpu.SMEM), IN_VMEM, IN_VMEM],
-    )(lax.axis_index("c").reshape(1), mine, other)
+    )(place, mine, other)
     arrived = lax.all_to_all(partial, ROWS, 0, 0, tiled=True)
     image, sums = kernel_call(
         sums_kernel,
         (shape((rhs, width), f32), shape((lax.axis_size(SUM_1), 2, LANES), f32)),
         "sums",
-    )(arrived, direction, residual)
+    )(arrived, own, direction, residual)
     sums = lax.all_to_all(sums, SUM_1, 0, 0, tiled=True)
     sums = kernel_call(middle_kernel, shape((lax.axis_size(SUM_2), 2, LANES), f32), "middle")(sums)
     sums = lax.all_to_all(sums, SUM_2, 0, 0, tiled=True)

time: 90.8 us -> 89.3 us (0.983)
  blocking collectives: 58.2 us -> 56.6 us
where the time goes in v5:
time: 89.3 us; the launch traced here: 88.9 us
  blocking collectives  56.6 us (63%)
  starting transfers between devices  19.9 us (22%)
  Pallas kernels  8.86 us (10%)
  waiting for transfers between devices  1.97 us (2%)
    ppermute x1, starting transfers between devices, local(): other = lax.ppermute(mine, 'c', [(0, 1), (1, 0)])  19.9 us
    all_to_all x1, blocking collectives, local(): sums = lax.all_to_all(sums, SUM_2, 0, 0, tiled=True)  12.8 us
    all_to_all x1, blocking collectives, local(): mine = lax.all_to_all(mine, ALL, 0, 0, axis_index_groups=groups, tiled=True)  12.3 us
    all_to_all x1, blocking collectives, local(): sums = lax.all_to_all(sums, SUM_1, 0, 0, tiled=True)  12.1 us
    all_to_all x1, blocking collectives, local(): arrived = lax.all_to_all(partial, ROWS, 0, 0, tiled=True)  11 us
    all_gather x1, blocking collectives, local(): lax.all_gather(jnp.pad(both, ((0, -both.shape[0] % 8), (0, 0))), 'c', axi...  8.38 us
    pallas_call x1, Pallas kernels, local(): kernel_call(product_kernel, (shape((peers, rhs, width), bf16), shape((rhs...  7.96 us
    ppermute x1, waiting for transfers between devices, local(): other = lax.ppermute(mine, 'c', [(0, 1), (1, 0)])  1.97 us
  transfers between devices with their start and end apart: 1, of which 1 were waited for; matrix products, arithmetic and copies ran while one was open for 0% of the time, Pallas kernels for 0%

profile of v5, /device:TPU:1, one launch (start us, length us, event | category | flops | bytes accessed | tf_op | source)
XLA Modules:
  0.0 88.9 jit_solution(6231621518466669847)
XLA Ops:
  0.6 0.0 copy-start.3
  0.6 0.7 convert_element_type.5
  1.4 0.0 copy-done.3
  1.4 8.4 %all_gather.3 = bf16[208,128]{1,0:T(8,128)(2,1)S(1)} all-gather(bf16[104,128]{1,0:T(8,128)(2,1)S(1)} %fusion.2), channel_id=1, replica_groups=mesh['yh'=4,'yl'=2,'zh'=4,'x'=4,'zl'=2,'c'=2] {'c'}, dimensions={0}, use_global_device_ids=true | all-gather | bytes 79872 | tf_op jit(solution)/shard_map/all_gather | solution.py:194
  9.8 0.1 broadcast_in_dim.8
  9.9 12.3 %all_to_all.20.mine_ref = bf16[32,104,128]{2,1,0:T(8,128)(2,1)S(1)} all-to-all(bf16[32,104,128]{2,1,0:T(8,128)(2,1)S(1)} %bitcast.3), channel_id=1, replica_groups={{0,16,32,48,128,144,160,176,256,272,288,304,384,400,416,432},{2,18,34,5..., dimensions={0} | all-to-all | bytes 1703936 | tf_op jit(solution)/shard_map/all_to_all | solution.py:197
  22.2 19.9 %collective-permute-start = (bf16[32,104,128]{2,1,0:T(8,128)(2,1)S(1)}, bf16[32,104,128]{2,1,0:T(8,128)(2,1)S(1)}, u32[]{:S(2)}, u32[]{:S(2)}) collective-permute-start(bf16[32,104,128]{2,1,0:T(8,128)(2,1)S(1)} %all_to_all.20.mine_ref), channel_id=1, source_target_pairs={{0,1},{1,0},{2,3},{3,2},{4,5},{5,4},{6,7},{7,6},{8,9},{9,8},{10,11... | collective-permute-start | bytes 2555912 | tf_op jit(solution)/shard_map/ppermute | solution.py:198
  42.1 2.0 %collective-permute-done.other_ref = bf16[32,104,128]{2,1,0:T(8,128)(2,1)S(1)} collective-permute-done((bf16[32,104,128]{2,1,0:T(8,128)(2,1)S(1)}, bf16[32,104,128]{2,1,0:T(8,128)(2,1)S(1)}, u32[]{:S(2)}, u32[]{:S(2)}) %collective-permute-start) | collective-permute-done | bytes 852000 | tf_op jit(solution)/shard_map/ppermute | solution.py:198
  44.1 8.0 %products.1 = (bf16[16,33,128]{2,1,0:T(8,128)(2,1)S(1)}, f32[33,128]{1,0:T(8,128)S(1)}) custom-call(s32[1]{0:T(128)} %bitcast.place_ref, bf16[32,104,128]{2,1,0:T(8,128)(2,1)S(1)} %all_to_all.20.mine_ref, bf16[32,104,128]{2,1,0:T(8,128)(2,1)S(1)} %collective-permute-done.other_ref), custom_call_target="tpu_custom_call" | custom-call | flops 2701131776 | bytes 152064 | tf_op jit(solution)/shard_map/products/pallas_call | solution.py:202
  52.0 0.0 copy-start
  52.0 0.0 copy-start.1
  52.0 11.0 %all_to_all.21.arrived_ref = bf16[16,33,128]{2,1,0:T(8,128)(2,1)S(1)} all-to-all(bf16[16,33,128]{2,1,0:T(8,128)(2,1)S(1)} %get-tuple-element.7), channel_id=1, replica_groups=mesh['yh'=4,'yl'=2,'zh'=4,'x'=4,'zl'=2,'c'=2] {'yl','x','zl'}, dimensions={0} | all-to-all | bytes 270336 | tf_op jit(solution)/shard_map/all_to_all | solution.py:215
  63.1 0.0 copy-done
  63.1 0.0 copy-done.1
  63.1 0.1 sums.1
  63.2 12.1 %all_to_all.22.arrived_ref = f32[16,2,128]{2,1,0:T(2,128)S(1)} all-to-all(f32[16,2,128]{2,1,0:T(2,128)S(1)} %get-tuple-element.9), channel_id=1, replica_groups=mesh['yh'=4,'yl'=2,'zh'=4,'x'=4,'zl'=2,'c'=2] {'zh','zl','c'}, dimensions={0} | all-to-all | bytes 32768 | tf_op jit(solution)/shard_map/all_to_all | solution.py:221
  75.3 0.0 copy-start.2
  75.3 12.8 %all_to_all.23.arrived_ref = f32[32,2,128]{2,1,0:T(2,128)S(1)} all-to-all(f32[32,2,128]{2,1,0:T(2,128)S(1)} %middle.1), channel_id=1, replica_groups=mesh['yh'=4,'yl'=2,'zh'=4,'x'=4,'zl'=2,'c'=2] {'yh','yl','x'}, dimensions={0} | all-to-all | bytes 65536 | tf_op jit(solution)/shard_map/all_to_all | solution.py:223
  88.1 0.0 copy-done.2
  88.1 0.7 last.1
  (2 shorter events, 0.0 us)
Async XLA Ops:
  0.6 0.7 copy-start.3
  22.2 21.8 %collective-permute-start = (bf16[32,104,128]{2,1,0:T(8,128)(2,1)S(1)}, bf16[32,104,128]{2,1,0:T(8,128)(2,1)S(1)}, u32[]{:S(2)}, u32[]{:S(2)}) collective-permute-start(bf16[32,104,128]{2,1,0:T(8,128)(2,1)S(1)} %all_to_all.20.mine_ref), channel_id=1, source_target_pairs={{0,1},{1,0},{2,3},{3,2},{4,5},{5,4},{6,7},{7,6},{8,9},{9,8},{10,11... | collective-permute-start | bytes 2555912 | tf_op jit(solution)/shard_map/ppermute | solution.py:198
  52.0 11.1 %copy-start = (f32[33,128]{1,0:T(8,128)S(1)}, f32[33,128]{1,0:T(8,128)}, u32[]{:S(2)}) copy-start(f32[33,128]{1,0:T(8,128)} %direction_ref.3) | copy-start | bytes 50692
  52.0 11.1 %copy-start.1 = (f32[33,128]{1,0:T(8,128)S(1)}, f32[33,128]{1,0:T(8,128)}, u32[]{:S(2)}) copy-start(f32[33,128]{1,0:T(8,128)} %residual_ref.3) | copy-start | bytes 50692
  75.3 12.8 %copy-start.2 = (f32[33,128]{1,0:T(8,128)S(1)}, f32[33,128]{1,0:T(8,128)}, u32[]{:S(2)}) copy-start(f32[33,128]{1,0:T(8,128)} %solution_ref.1) | copy-start | bytes 50692

commit v6 on v5

--- a/solution.py
+++ b/solution.py
@@ -13,11 +13,11 @@
 f32 = jnp.float32
 bf16 = jnp.bfloat16
 
-ALL = ("yh", "yl", "zh", "x", "zl", "c")
-SIZES = (4, 2, 4, 4, 2, 2)
-ROWS = ("yl", "x", "zl")
+ALL = ("y", "zh", "xh", "xl", "zl", "c")
+SIZES = (8, 4, 2, 2, 2, 2)
+ROWS = ('y', 'xl')
 SUM_1 = ("zh", "zl", "c")
-SUM_2 = ("yh", "yl", "x")
+SUM_2 = ("y", "xh", "xl")
 
 amplitude = 1.0
 decay_rate = 1.0 / 16.0
@@ -64,8 +64,8 @@
 
 def far_and_near():
     at = np.arange(math.prod(SIZES)).reshape(SIZES)
-    far = at[..., 0].transpose(1, 3, 4, 0, 2).reshape(-1, SIZES[0] * SIZES[2])
-    near = at[..., 1].transpose(0, 2, 1, 3, 4).reshape(far.shape)
+    far = at[..., 0].transpose(0, 3, 1, 4, 2).reshape(-1, 16)
+    near = at[..., 1].transpose(1, 4, 2, 0, 3).reshape(far.shape)
     return np.concatenate([far, near]).tolist()
 
 

time: 89.3 us -> 88.7 us (level)
  starting transfers between devices: 19.9 us -> 9.45 us
  blocking collectives: 56.6 us -> 66.4 us
    ppermute x1, starting transfers between devices: 19.9 us -> 9.45 us  [local(): other = lax.ppermute(mine, 'c', [(0, 1), (1, 0)])]
    all_to_all x1, blocking collectives: 12.3 us -> 18.5 us  [local(): mine = lax.all_to_all(mine, ALL, 0, 0, axis_index_groups=groups, tiled=True)]
    all_to_all x1, blocking collectives: 11 us -> 15.8 us  [local(): arrived = lax.all_to_all(partial, ROWS, 0, 0, tiled=True)]
    all_to_all x1, blocking collectives: 12.8 us -> 11.7 us  [local(): sums = lax.all_to_all(sums, SUM_2, 0, 0, tiled=True)]
where the time goes in v6:
time: 88.7 us; the launch traced here: 88.2 us
  blocking collectives  66.4 us (75%)
  starting transfers between devices  9.45 us (11%)
  Pallas kernels  8.87 us (10%)
  waiting for transfers between devices  1.98 us (2%)
    all_to_all x1, blocking collectives, local(): mine = lax.all_to_all(mine, ALL, 0, 0, axis_index_groups=groups, tiled=True)  18.5 us
    all_to_all x1, blocking collectives, local(): arrived = lax.all_to_all(partial, ROWS, 0, 0, tiled=True)  15.8 us
    all_to_all x1, blocking collectives, local(): sums = lax.all_to_all(sums, SUM_1, 0, 0, tiled=True)  11.9 us
    all_to_all x1, blocking collectives, local(): sums = lax.all_to_all(sums, SUM_2, 0, 0, tiled=True)  11.7 us
    ppermute x1, starting transfers between devices, local(): other = lax.ppermute(mine, 'c', [(0, 1), (1, 0)])  9.45 us
    all_gather x1, blocking collectives, local(): lax.all_gather(jnp.pad(both, ((0, -both.shape[0] % 8), (0, 0))), 'c', axi...  8.38 us
    pallas_call x1, Pallas kernels, local(): kernel_call(product_kernel, (shape((peers, rhs, width), bf16), shape((rhs...  7.96 us
    ppermute x1, waiting for transfers between devices, local(): other = lax.ppermute(mine, 'c', [(0, 1), (1, 0)])  1.98 us
  transfers between devices with their start and end apart: 1, of which 1 were waited for; matrix products, arithmetic and copies ran while one was open for 0% of the time, Pallas kernels for 0%

profile of v6, /device:TPU:1, one launch (start us, length us, event | category | flops | bytes accessed | tf_op | source)
XLA Modules:
  0.0 88.2 jit_solution(9103226623203556646)
XLA Ops:
  0.6 0.0 copy-start.3
  0.6 0.7 convert_element_type.5
  1.4 0.0 copy-done.3
  1.4 8.4 %all_gather.3 = bf16[208,128]{1,0:T(8,128)(2,1)S(1)} all-gather(bf16[104,128]{1,0:T(8,128)(2,1)S(1)} %fusion.2), channel_id=1, replica_groups=mesh['y'=8,'zh'=4,'xh'=2,'xl'=2,'zl'=2,'c'=2] {'c'}, dimensions={0}, use_global_device_ids=true | all-gather | bytes 79872 | tf_op jit(solution)/shard_map/all_gather | solution.py:194
  9.8 0.1 broadcast_in_dim.8
  9.9 18.5 %all_to_all.20.mine_ref = bf16[32,104,128]{2,1,0:T(8,128)(2,1)S(1)} all-to-all(bf16[32,104,128]{2,1,0:T(8,128)(2,1)S(1)} %bitcast.3), channel_id=1, replica_groups={{0,8,2,10,16,24,18,26,32,40,34,42,48,56,50,58},{4,12,6,14,20,28,22,30,3..., dimensions={0} | all-to-all | bytes 1703936 | tf_op jit(solution)/shard_map/all_to_all | solution.py:197
  28.4 9.5 %collective-permute-start = (bf16[32,104,128]{2,1,0:T(8,128)(2,1)S(1)}, bf16[32,104,128]{2,1,0:T(8,128)(2,1)S(1)}, u32[]{:S(2)}, u32[]{:S(2)}) collective-permute-start(bf16[32,104,128]{2,1,0:T(8,128)(2,1)S(1)} %all_to_all.20.mine_ref), channel_id=1, source_target_pairs={{0,1},{1,0},{2,3},{3,2},{4,5},{5,4},{6,7},{7,6},{8,9},{9,8},{10,11... | collective-permute-start | bytes 2555912 | tf_op jit(solution)/shard_map/ppermute | solution.py:198
  37.9 2.0 %collective-permute-done.other_ref = bf16[32,104,128]{2,1,0:T(8,128)(2,1)S(1)} collective-permute-done((bf16[32,104,128]{2,1,0:T(8,128)(2,1)S(1)}, bf16[32,104,128]{2,1,0:T(8,128)(2,1)S(1)}, u32[]{:S(2)}, u32[]{:S(2)}) %collective-permute-start) | collective-permute-done | bytes 852000 | tf_op jit(solution)/shard_map/ppermute | solution.py:198
  39.9 8.0 %products.1 = (bf16[16,33,128]{2,1,0:T(8,128)(2,1)S(1)}, f32[33,128]{1,0:T(8,128)S(1)}) custom-call(s32[1]{0:T(128)} %bitcast.place_ref, bf16[32,104,128]{2,1,0:T(8,128)(2,1)S(1)} %all_to_all.20.mine_ref, bf16[32,104,128]{2,1,0:T(8,128)(2,1)S(1)} %collective-permute-done.other_ref), custom_call_target="tpu_custom_call" | custom-call | flops 2701131776 | bytes 152064 | tf_op jit(solution)/shard_map/products/pallas_call | solution.py:202
  47.8 0.0 copy-start
  47.9 0.0 copy-start.1
  47.9 15.8 %all_to_all.21.arrived_ref = bf16[16,33,128]{2,1,0:T(8,128)(2,1)S(1)} all-to-all(bf16[16,33,128]{2,1,0:T(8,128)(2,1)S(1)} %get-tuple-element.7), channel_id=1, replica_groups=mesh['y'=8,'zh'=4,'xh'=2,'xl'=2,'zl'=2,'c'=2] {'y','xl'}, dimensions={0} | all-to-all | bytes 270336 | tf_op jit(solution)/shard_map/all_to_all | solution.py:215
  63.7 0.0 copy-done
  63.7 0.0 copy-done.1
  63.7 0.1 sums.1
  63.9 11.9 %all_to_all.22.arrived_ref = f32[16,2,128]{2,1,0:T(2,128)S(1)} all-to-all(f32[16,2,128]{2,1,0:T(2,128)S(1)} %get-tuple-element.9), channel_id=1, replica_groups=mesh['y'=8,'zh'=4,'xh'=2,'xl'=2,'zl'=2,'c'=2] {'zh','zl','c'}, dimensions={0} | all-to-all | bytes 32768 | tf_op jit(solution)/shard_map/all_to_all | solution.py:221
  75.8 0.0 copy-start.2
  75.8 11.7 %all_to_all.23.arrived_ref = f32[32,2,128]{2,1,0:T(2,128)S(1)} all-to-all(f32[32,2,128]{2,1,0:T(2,128)S(1)} %middle.1), channel_id=1, replica_groups=mesh['y'=8,'zh'=4,'xh'=2,'xl'=2,'zl'=2,'c'=2] {'y','xh','xl'}, dimensions={0} | all-to-all | bytes 65536 | tf_op jit(solution)/shard_map/all_to_all | solution.py:223
  87.5 0.0 copy-done.2
  87.5 0.7 last.1
  (2 shorter events, 0.0 us)
Async XLA Ops:
  0.6 0.7 copy-start.3
  28.4 11.4 %collective-permute-start = (bf16[32,104,128]{2,1,0:T(8,128)(2,1)S(1)}, bf16[32,104,128]{2,1,0:T(8,128)(2,1)S(1)}, u32[]{:S(2)}, u32[]{:S(2)}) collective-permute-start(bf16[32,104,128]{2,1,0:T(8,128)(2,1)S(1)} %all_to_all.20.mine_ref), channel_id=1, source_target_pairs={{0,1},{1,0},{2,3},{3,2},{4,5},{5,4},{6,7},{7,6},{8,9},{9,8},{10,11... | collective-permute-start | bytes 2555912 | tf_op jit(solution)/shard_map/ppermute | solution.py:198
  47.8 15.9 %copy-start = (f32[33,128]{1,0:T(8,128)S(1)}, f32[33,128]{1,0:T(8,128)}, u32[]{:S(2)}) copy-start(f32[33,128]{1,0:T(8,128)} %direction_ref.3) | copy-start | bytes 50692
  47.9 15.9 %copy-start.1 = (f32[33,128]{1,0:T(8,128)S(1)}, f32[33,128]{1,0:T(8,128)}, u32[]{:S(2)}) copy-start(f32[33,128]{1,0:T(8,128)} %residual_ref.3) | copy-start | bytes 50692
  75.8 11.7 %copy-start.2 = (f32[33,128]{1,0:T(8,128)S(1)}, f32[33,128]{1,0:T(8,128)}, u32[]{:S(2)}) copy-start(f32[33,128]{1,0:T(8,128)} %solution_ref.1) | copy-start | bytes 50692

commit v7 on v6

--- a/solution.py
+++ b/solution.py
@@ -15,7 +15,7 @@
 
 ALL = ("y", "zh", "xh", "xl", "zl", "c")
 SIZES = (8, 4, 2, 2, 2, 2)
-ROWS = ('y', 'xl')
+ROWS = ('zh', 'zl', 'xl')
 SUM_1 = ("zh", "zl", "c")
 SUM_2 = ("y", "xh", "xl")
 
@@ -64,8 +64,8 @@
 
 def far_and_near():
     at = np.arange(math.prod(SIZES)).reshape(SIZES)
-    far = at[..., 0].transpose(0, 3, 1, 4, 2).reshape(-1, 16)
-    near = at[..., 1].transpose(1, 4, 2, 0, 3).reshape(far.shape)
+    far = at[..., 0].transpose(1, 4, 3, 0, 2).reshape(-1, 16)
+    near = at[..., 1].transpose(0, 2, 1, 4, 3).reshape(far.shape)
     return np.concatenate([far, near]).tolist()
 
 

time: 88.7 us -> 88.7 us (level)
  starting transfers between devices: 9.45 us -> 3.2 us
  blocking collectives: 66.4 us -> 72.6 us
    ppermute x1, starting transfers between devices: 9.45 us -> 3.2 us  [local(): other = lax.ppermute(mine, 'c', [(0, 1), (1, 0)])]
    all_to_all x1, blocking collectives: 15.8 us -> 19.1 us  [local(): arrived = lax.all_to_all(partial, ROWS, 0, 0, tiled=True)]
    all_to_all x1, blocking collectives: 18.5 us -> 21.6 us  [local(): mine = lax.all_to_all(mine, ALL, 0, 0, axis_index_groups=groups, tiled=True)]
where the time goes in v7:
time: 88.7 us; the launch traced here: 88.3 us
  blocking collectives  72.6 us (82%)
  Pallas kernels  8.87 us (10%)
  starting transfers between devices  3.2 us (4%)
  waiting for transfers between devices  1.97 us (2%)
    all_to_all x1, blocking collectives, local(): mine = lax.all_to_all(mine, ALL, 0, 0, axis_index_groups=groups, tiled=True)  21.6 us
    all_to_all x1, blocking collectives, local(): arrived = lax.all_to_all(partial, ROWS, 0, 0, tiled=True)  19.1 us
    all_to_all x1, blocking collectives, local(): sums = lax.all_to_all(sums, SUM_1, 0, 0, tiled=True)  11.9 us
    all_to_all x1, blocking collectives, local(): sums = lax.all_to_all(sums, SUM_2, 0, 0, tiled=True)  11.7 us
    all_gather x1, blocking collectives, local(): lax.all_gather(jnp.pad(both, ((0, -both.shape[0] % 8), (0, 0))), 'c', axi...  8.38 us
    pallas_call x1, Pallas kernels, local(): kernel_call(product_kernel, (shape((peers, rhs, width), bf16), shape((rhs...  7.97 us
    ppermute x1, starting transfers between devices, local(): other = lax.ppermute(mine, 'c', [(0, 1), (1, 0)])  3.2 us
    ppermute x1, waiting for transfers between devices, local(): other = lax.ppermute(mine, 'c', [(0, 1), (1, 0)])  1.97 us
  transfers between devices with their start and end apart: 1, of which 1 were waited for; matrix products, arithmetic and copies ran while one was open for 0% of the time, Pallas kernels for 0%

profile of v7, /device:TPU:1, one launch (start us, length us, event | category | flops | bytes accessed | tf_op | source)
XLA Modules:
  0.0 88.3 jit_solution(12500253079956819196)
XLA Ops:
  0.6 0.0 copy-start.3
  0.6 0.7 convert_element_type.5
  1.4 0.0 copy-done.3
  1.4 8.4 %all_gather.3 = bf16[208,128]{1,0:T(8,128)(2,1)S(1)} all-gather(bf16[104,128]{1,0:T(8,128)(2,1)S(1)} %fusion.2), channel_id=1, replica_groups=mesh['y'=8,'zh'=4,'xh'=2,'xl'=2,'zl'=2,'c'=2] {'c'}, dimensions={0}, use_global_device_ids=true | all-gather | bytes 79872 | tf_op jit(solution)/shard_map/all_gather | solution.py:194
  9.8 0.1 broadcast_in_dim.8
  9.9 21.6 %all_to_all.20.mine_ref = bf16[32,104,128]{2,1,0:T(8,128)(2,1)S(1)} all-to-all(bf16[32,104,128]{2,1,0:T(8,128)(2,1)S(1)} %bitcast.3), channel_id=1, replica_groups={{0,8,64,72,128,136,192,200,256,264,320,328,384,392,448,456},{4,12,68,76..., dimensions={0} | all-to-all | bytes 1703936 | tf_op jit(solution)/shard_map/all_to_all | solution.py:197
  31.5 3.2 %collective-permute-start = (bf16[32,104,128]{2,1,0:T(8,128)(2,1)S(1)}, bf16[32,104,128]{2,1,0:T(8,128)(2,1)S(1)}, u32[]{:S(2)}, u32[]{:S(2)}) collective-permute-start(bf16[32,104,128]{2,1,0:T(8,128)(2,1)S(1)} %all_to_all.20.mine_ref), channel_id=1, source_target_pairs={{0,1},{1,0},{2,3},{3,2},{4,5},{5,4},{6,7},{7,6},{8,9},{9,8},{10,11... | collective-permute-start | bytes 2555912 | tf_op jit(solution)/shard_map/ppermute | solution.py:198
  34.7 2.0 %collective-permute-done.other_ref = bf16[32,104,128]{2,1,0:T(8,128)(2,1)S(1)} collective-permute-done((bf16[32,104,128]{2,1,0:T(8,128)(2,1)S(1)}, bf16[32,104,128]{2,1,0:T(8,128)(2,1)S(1)}, u32[]{:S(2)}, u32[]{:S(2)}) %collective-permute-start) | collective-permute-done | bytes 852000 | tf_op jit(solution)/shard_map/ppermute | solution.py:198
  36.7 8.0 %products.1 = (bf16[16,33,128]{2,1,0:T(8,128)(2,1)S(1)}, f32[33,128]{1,0:T(8,128)S(1)}) custom-call(s32[1]{0:T(128)} %bitcast.place_ref, bf16[32,104,128]{2,1,0:T(8,128)(2,1)S(1)} %all_to_all.20.mine_ref, bf16[32,104,128]{2,1,0:T(8,128)(2,1)S(1)} %collective-permute-done.other_ref), custom_call_target="tpu_custom_call" | custom-call | flops 2701131776 | bytes 152064 | tf_op jit(solution)/shard_map/products/pallas_call | solution.py:202
  44.6 0.0 copy-start
  44.6 0.0 copy-start.1
  44.7 19.1 %all_to_all.21.arrived_ref = bf16[16,33,128]{2,1,0:T(8,128)(2,1)S(1)} all-to-all(bf16[16,33,128]{2,1,0:T(8,128)(2,1)S(1)} %get-tuple-element.7), channel_id=1, replica_groups=mesh['y'=8,'zh'=4,'xh'=2,'xl'=2,'zl'=2,'c'=2] {'zh','zl','xl'}, dimensions={0} | all-to-all | bytes 270336 | tf_op jit(solution)/shard_map/all_to_all | solution.py:215
  63.8 0.0 copy-done
  63.8 0.0 copy-done.1
  63.8 0.1 sums.1
  63.9 11.9 %all_to_all.22.arrived_ref = f32[16,2,128]{2,1,0:T(2,128)S(1)} all-to-all(f32[16,2,128]{2,1,0:T(2,128)S(1)} %get-tuple-element.9), channel_id=1, replica_groups=mesh['y'=8,'zh'=4,'xh'=2,'xl'=2,'zl'=2,'c'=2] {'zh','zl','c'}, dimensions={0} | all-to-all | bytes 32768 | tf_op jit(solution)/shard_map/all_to_all | solution.py:221
  75.8 0.0 copy-start.2
  75.8 11.7 %all_to_all.23.arrived_ref = f32[32,2,128]{2,1,0:T(2,128)S(1)} all-to-all(f32[32,2,128]{2,1,0:T(2,128)S(1)} %middle.1), channel_id=1, replica_groups=mesh['y'=8,'zh'=4,'xh'=2,'xl'=2,'zl'=2,'c'=2] {'y','xh','xl'}, dimensions={0} | all-to-all | bytes 65536 | tf_op jit(solution)/shard_map/all_to_all | solution.py:223
  87.5 0.0 copy-done.2
  87.5 0.7 last.1
  (2 shorter events, 0.0 us)
Async XLA Ops:
  0.6 0.7 copy-start.3
  31.5 5.2 %collective-permute-start = (bf16[32,104,128]{2,1,0:T(8,128)(2,1)S(1)}, bf16[32,104,128]{2,1,0:T(8,128)(2,1)S(1)}, u32[]{:S(2)}, u32[]{:S(2)}) collective-permute-start(bf16[32,104,128]{2,1,0:T(8,128)(2,1)S(1)} %all_to_all.20.mine_ref), channel_id=1, source_target_pairs={{0,1},{1,0},{2,3},{3,2},{4,5},{5,4},{6,7},{7,6},{8,9},{9,8},{10,11... | collective-permute-start | bytes 2555912 | tf_op jit(solution)/shard_map/ppermute | solution.py:198
  44.6 19.1 %copy-start = (f32[33,128]{1,0:T(8,128)S(1)}, f32[33,128]{1,0:T(8,128)}, u32[]{:S(2)}) copy-start(f32[33,128]{1,0:T(8,128)} %direction_ref.3) | copy-start | bytes 50692
  44.6 19.1 %copy-start.1 = (f32[33,128]{1,0:T(8,128)S(1)}, f32[33,128]{1,0:T(8,128)}, u32[]{:S(2)}) copy-start(f32[33,128]{1,0:T(8,128)} %residual_ref.3) | copy-start | bytes 50692
  75.8 11.7 %copy-start.2 = (f32[33,128]{1,0:T(8,128)S(1)}, f32[33,128]{1,0:T(8,128)}, u32[]{:S(2)}) copy-start(f32[33,128]{1,0:T(8,128)} %solution_ref.1) | copy-start | bytes 50692

commit v8 on v6

--- a/solution.py
+++ b/solution.py
@@ -64,13 +64,13 @@
 
 def far_and_near():
     at = np.arange(math.prod(SIZES)).reshape(SIZES)
-    far = at[..., 0].transpose(0, 3, 1, 4, 2).reshape(-1, 16)
-    near = at[..., 1].transpose(1, 4, 2, 0, 3).reshape(far.shape)
+    far = at[..., 1].transpose(0, 3, 1, 4, 2).reshape(-1, 16)
+    near = at[..., 0].transpose(1, 4, 2, 0, 3).reshape(far.shape)
     return np.concatenate([far, near]).tolist()
 
 
 def product_kernel(place_ref, mine_ref, other_ref, out_ref, own_ref, row_side, col_side, dirs, parts):
-    first = lax.rem(place_ref[0], 2) == 0
+    first = lax.rem(place_ref[0], 2) == 1
     me = lax.div(place_ref[0], 2)
     rhs = dirs.shape[0]
     dim = DEPTH // 2
@@ -79,7 +79,7 @@
     per_step = ROW_BLOCK // LANES
 
     def prepare_rows(k):
-        x = jnp.where(first, other_ref[2 * k][0:dim], mine_ref[2 * k + 1][0:dim])
+        x = jnp.where(first, other_ref[2 * k + 1][0:dim], mine_ref[2 * k][0:dim])
         here = slice(k * LANES, (k + 1) * LANES)
         row_side[0:dim, here] = (x.astype(f32) * (2.0 * decay_rate)).astype(bf16)
         row_side[dim:DEPTH, here] = norm_features(x, 0)

time: 88.7 us -> 87.7 us (0.989)
  starting transfers between devices: 9.45 us -> 1.91 us
  blocking collectives: 66.4 us -> 72.6 us
    ppermute x1, starting transfers between devices: 9.45 us -> 1.91 us  [local(): other = lax.ppermute(mine, 'c', [(0, 1), (1, 0)])]
    all_to_all x1, blocking collectives: 18.5 us -> 24.3 us  [local(): mine = lax.all_to_all(mine, ALL, 0, 0, axis_index_groups=groups, tiled=True)]
where the time goes in v8:
time: 87.7 us; the launch traced here: 87.3 us
  blocking collectives  72.6 us (83%)
  Pallas kernels  8.86 us (10%)
  waiting for transfers between devices  2.34 us (3%)
  starting transfers between devices  1.91 us (2%)
    all_to_all x1, blocking collectives, local(): mine = lax.all_to_all(mine, ALL, 0, 0, axis_index_groups=groups, tiled=True)  24.3 us
    all_to_all x1, blocking collectives, local(): arrived = lax.all_to_all(partial, ROWS, 0, 0, tiled=True)  16 us
    all_to_all x1, blocking collectives, local(): sums = lax.all_to_all(sums, SUM_1, 0, 0, tiled=True)  12.2 us
    all_to_all x1, blocking collectives, local(): sums = lax.all_to_all(sums, SUM_2, 0, 0, tiled=True)  11.7 us
    all_gather x1, blocking collectives, local(): lax.all_gather(jnp.pad(both, ((0, -both.shape[0] % 8), (0, 0))), 'c', axi...  8.38 us
    pallas_call x1, Pallas kernels, local(): kernel_call(product_kernel, (shape((peers, rhs, width), bf16), shape((rhs...  7.96 us
    ppermute x1, waiting for transfers between devices, local(): other = lax.ppermute(mine, 'c', [(0, 1), (1, 0)])  2.34 us
    ppermute x1, starting transfers between devices, local(): other = lax.ppermute(mine, 'c', [(0, 1), (1, 0)])  1.91 us
  transfers between devices with their start and end apart: 1, of which 1 were waited for; matrix products, arithmetic and copies ran while one was open for 0% of the time, Pallas kernels for 0%

profile of v8, /device:TPU:1, one launch (start us, length us, event | category | flops | bytes accessed | tf_op | source)
XLA Modules:
  0.0 87.3 jit_solution(17569033592149338762)
XLA Ops:
  0.6 0.0 copy-start.3
  0.6 0.7 convert_element_type.5
  1.4 0.0 copy-done.3
  1.4 8.4 %all_gather.3 = bf16[208,128]{1,0:T(8,128)(2,1)S(1)} all-gather(bf16[104,128]{1,0:T(8,128)(2,1)S(1)} %fusion.2), channel_id=1, replica_groups=mesh['y'=8,'zh'=4,'xh'=2,'xl'=2,'zl'=2,'c'=2] {'c'}, dimensions={0}, use_global_device_ids=true | all-gather | bytes 79872 | tf_op jit(solution)/shard_map/all_gather | solution.py:194
  9.8 0.1 broadcast_in_dim.8
  9.9 24.3 %all_to_all.20.mine_ref = bf16[32,104,128]{2,1,0:T(8,128)(2,1)S(1)} all-to-all(bf16[32,104,128]{2,1,0:T(8,128)(2,1)S(1)} %bitcast.3), channel_id=1, replica_groups={{1,9,3,11,17,25,19,27,33,41,35,43,49,57,51,59},{5,13,7,15,21,29,23,31,3..., dimensions={0} | all-to-all | bytes 1703936 | tf_op jit(solution)/shard_map/all_to_all | solution.py:197
  34.2 1.9 %collective-permute-start = (bf16[32,104,128]{2,1,0:T(8,128)(2,1)S(1)}, bf16[32,104,128]{2,1,0:T(8,128)(2,1)S(1)}, u32[]{:S(2)}, u32[]{:S(2)}) collective-permute-start(bf16[32,104,128]{2,1,0:T(8,128)(2,1)S(1)} %all_to_all.20.mine_ref), channel_id=1, source_target_pairs={{0,1},{1,0},{2,3},{3,2},{4,5},{5,4},{6,7},{7,6},{8,9},{9,8},{10,11... | collective-permute-start | bytes 2555912 | tf_op jit(solution)/shard_map/ppermute | solution.py:198
  36.1 2.3 %collective-permute-done.other_ref = bf16[32,104,128]{2,1,0:T(8,128)(2,1)S(1)} collective-permute-done((bf16[32,104,128]{2,1,0:T(8,128)(2,1)S(1)}, bf16[32,104,128]{2,1,0:T(8,128)(2,1)S(1)}, u32[]{:S(2)}, u32[]{:S(2)}) %collective-permute-start) | collective-permute-done | bytes 852000 | tf_op jit(solution)/shard_map/ppermute | solution.py:198
  38.5 8.0 %products.1 = (bf16[16,33,128]{2,1,0:T(8,128)(2,1)S(1)}, f32[33,128]{1,0:T(8,128)S(1)}) custom-call(s32[1]{0:T(128)} %bitcast.place_ref, bf16[32,104,128]{2,1,0:T(8,128)(2,1)S(1)} %all_to_all.20.mine_ref, bf16[32,104,128]{2,1,0:T(8,128)(2,1)S(1)} %collective-permute-done.other_ref), custom_call_target="tpu_custom_call" | custom-call | flops 2701131776 | bytes 152064 | tf_op jit(solution)/shard_map/products/pallas_call | solution.py:202
  46.4 0.0 copy-start
  46.5 0.0 copy-start.1
  46.5 16.0 %all_to_all.21.arrived_ref = bf16[16,33,128]{2,1,0:T(8,128)(2,1)S(1)} all-to-all(bf16[16,33,128]{2,1,0:T(8,128)(2,1)S(1)} %get-tuple-element.7), channel_id=1, replica_groups=mesh['y'=8,'zh'=4,'xh'=2,'xl'=2,'zl'=2,'c'=2] {'y','xl'}, dimensions={0} | all-to-all | bytes 270336 | tf_op jit(solution)/shard_map/all_to_all | solution.py:215
  62.5 0.0 copy-done
  62.5 0.0 copy-done.1
  62.5 0.1 sums.1
  62.6 12.2 %all_to_all.22.arrived_ref = f32[16,2,128]{2,1,0:T(2,128)S(1)} all-to-all(f32[16,2,128]{2,1,0:T(2,128)S(1)} %get-tuple-element.9), channel_id=1, replica_groups=mesh['y'=8,'zh'=4,'xh'=2,'xl'=2,'zl'=2,'c'=2] {'zh','zl','c'}, dimensions={0} | all-to-all | bytes 32768 | tf_op jit(solution)/shard_map/all_to_all | solution.py:221
  74.9 0.0 copy-start.2
  74.9 11.7 %all_to_all.23.arrived_ref = f32[32,2,128]{2,1,0:T(2,128)S(1)} all-to-all(f32[32,2,128]{2,1,0:T(2,128)S(1)} %middle.1), channel_id=1, replica_groups=mesh['y'=8,'zh'=4,'xh'=2,'xl'=2,'zl'=2,'c'=2] {'y','xh','xl'}, dimensions={0} | all-to-all | bytes 65536 | tf_op jit(solution)/shard_map/all_to_all | solution.py:223
  86.5 0.0 copy-done.2
  86.6 0.7 last.1
  (2 shorter events, 0.0 us)
Async XLA Ops:
  0.6 0.7 copy-start.3
  34.2 4.3 %collective-permute-start = (bf16[32,104,128]{2,1,0:T(8,128)(2,1)S(1)}, bf16[32,104,128]{2,1,0:T(8,128)(2,1)S(1)}, u32[]{:S(2)}, u32[]{:S(2)}) collective-permute-start(bf16[32,104,128]{2,1,0:T(8,128)(2,1)S(1)} %all_to_all.20.mine_ref), channel_id=1, source_target_pairs={{0,1},{1,0},{2,3},{3,2},{4,5},{5,4},{6,7},{7,6},{8,9},{9,8},{10,11... | collective-permute-start | bytes 2555912 | tf_op jit(solution)/shard_map/ppermute | solution.py:198
  46.4 16.1 %copy-start = (f32[33,128]{1,0:T(8,128)S(1)}, f32[33,128]{1,0:T(8,128)}, u32[]{:S(2)}) copy-start(f32[33,128]{1,0:T(8,128)} %direction_ref.3) | copy-start | bytes 50692
  46.5 16.1 %copy-start.1 = (f32[33,128]{1,0:T(8,128)S(1)}, f32[33,128]{1,0:T(8,128)}, u32[]{:S(2)}) copy-start(f32[33,128]{1,0:T(8,128)} %residual_ref.3) | copy-start | bytes 50692
  74.9 11.7 %copy-start.2 = (f32[33,128]{1,0:T(8,128)S(1)}, f32[33,128]{1,0:T(8,128)}, u32[]{:S(2)}) copy-start(f32[33,128]{1,0:T(8,128)} %solution_ref.1) | copy-start | bytes 50692
